TPU v7x, 128 devices: a whole 4x4x4 slice. The times are simulated.
128 devices in a mesh: group: 4 (over x), sector: 32 (over y, z, core).
Axes of the slice: x: 4, y: 4, z: 4, core: 2. Of those that a mesh axis runs over, the one named last changes fastest.
Arguments:
- state: float32 [128, 128, 4, 128], P(('group', 'sector')), may hold values from -180 to 180
- panel: bfloat16 [32, 32, 256], P('group'), may hold values from -3 to 3
- left_env: bfloat16 [128, 32, 128, 128], P(('group', 'sector')), may hold values from -1.5 to 1.5
- right_env: bfloat16 [128, 32, 128, 128], P(('group', 'sector')), may hold values from -1 to 1
- left_match: int32 [128], P(('group', 'sector')), may hold values from 0 to 31
- right_match: int32 [128], P(('group', 'sector')), may hold values from 0 to 31
- phys_states: int32 [128, 4], P(('group', 'sector')), may hold values from 0 to 15, all different within a row
Outputs:
- new_state: float32 [128, 128, 4, 128], P(('group', 'sector'))
- hessenberg: float32 [8, 8], replicated
Inputs may be any that keep to these rules, and one draw needn't show every extreme that they name: `left_match`: environment block index within the sector's own group, below 32. `right_match`: environment block index within the sector's own group, below 32. `phys_states`: each sector's 4 states are different.
All inputs are finite; a program needn't handle non-finite values.
Results may differ from a plain program's by a relative error of at most 0.025.
Values may be sent and summed in bfloat16 or wider, within the bound.
A program may use at most 128 MiB of HBM per device.

v0:
```python
import jax
import jax.numpy as jnp
from jax import lax
from jax.sharding import PartitionSpec as P

KRYLOV = 8


TAU = 3.0
EPS = 1e-06
HIGH = lax.Precision.HIGHEST


def select_mix(panel, states):
    pairs = states[:, None] * 16 + states[None, :]
    choose = (
        jnp.arange(panel.shape[2], dtype=jnp.int32)[None, None, :] == pairs[:, :, None]
    ).astype(jnp.bfloat16)
    mixed = jnp.einsum("acz,qpz->aqcp", panel, choose, preferred_element_type=jnp.float32)
    return mixed.astype(jnp.bfloat16)


def apply_sector(block_in, left_block, right_block, mixing):
    channels, size = (left_block.shape[0], left_block.shape[1])
    states = block_in.shape[1]
    inner = jnp.dot(
        left_block.reshape(channels * size, size),
        block_in.reshape(size, states * size),
        preferred_element_type=jnp.float32,
    )
    inner = inner.astype(jnp.bfloat16).reshape(channels, size, states, size)
    middle = jnp.einsum(
        "aiqj,aqcp->cipj", inner, mixing, preferred_element_type=jnp.float32
    ).astype(jnp.bfloat16)
    return jnp.einsum("cipj,crj->ipr", middle, right_block, preferred_element_type=jnp.float32)


def exponent_column(hessenberg):
    scaled = -TAU / 16.0 * hessenberg
    power_term = jnp.eye(hessenberg.shape[0], dtype=jnp.float32)
    series = power_term
    for order in range(1, 11):
        power_term = jnp.dot(power_term, scaled, precision=HIGH) / float(order)
        series = series + power_term
    for square in range(4):
        series = jnp.dot(series, series, precision=HIGH)
    return series[:, 0]


def local(state, panel, left_env, right_env, left_match, right_match, phys_states):
    owned, block_size, states = (state.shape[0], state.shape[1], state.shape[2])
    channels = left_env.shape[1]
    full_panel = lax.all_gather(panel, "group", axis=0, tiled=True)
    mixes = jax.vmap(lambda chosen: select_mix(full_panel, chosen))(phys_states)
    left_rows = left_env.reshape(owned, channels * block_size, block_size)
    right_rows = right_env.reshape(owned, channels * block_size, block_size)
    sector_count = lax.axis_size("sector")
    match_lists = (
        lax.all_gather(left_match, "sector", axis=0, tiled=True),
        lax.all_gather(right_match, "sector", axis=0, tiled=True),
    )
    left_index = match_lists[0].reshape(sector_count, owned).T
    right_index = match_lists[1].reshape(sector_count, owned).T
    spread = (
        lax.all_to_all(left_rows, "sector", split_axis=1, concat_axis=0, tiled=True),
        lax.all_to_all(right_rows, "sector", split_axis=1, concat_axis=0, tiled=True),
    )
    sends = (jnp.take(spread[0], left_index, axis=0), jnp.take(spread[1], right_index, axis=0))
    routed = (
        lax.all_to_all(sends[0], "sector", split_axis=1, concat_axis=1, tiled=True),
        lax.all_to_all(sends[1], "sector", split_axis=1, concat_axis=1, tiled=True),
    )
    left_blocks = routed[0]
    right_blocks = routed[1]
    flattened = state.reshape(-1)
    length = flattened.shape[0]
    start_sq = lax.psum(jnp.sum(flattened * flattened), ("group", "sector"))
    krylov_basis = (
        jnp.zeros((KRYLOV, length), jnp.float32).at[0].set(flattened / jnp.sqrt(start_sq + EPS))
    )
    hessenberg = jnp.zeros((KRYLOV, KRYLOV), jnp.float32)
    for column in range(KRYLOV):
        blocks = (
            krylov_basis[column].reshape(owned, block_size, states, block_size).astype(jnp.bfloat16)
        )
        applied = jax.vmap(apply_sector)(blocks, left_blocks, right_blocks, mixes).reshape(-1)
        local_projection = jnp.dot(krylov_basis, applied, precision=HIGH)
        projection = lax.psum(local_projection, ("group", "sector"))
        remainder = applied - jnp.dot(projection, krylov_basis, precision=HIGH)
        if column + 1 < KRYLOV:
            norm_sq = lax.psum(jnp.sum(remainder * remainder), ("group", "sector"))
        hessenberg = hessenberg.at[:, column].set(projection)
        if column + 1 < KRYLOV:
            subdiag = jnp.sqrt(norm_sq + EPS)
            hessenberg = hessenberg.at[column + 1, column].set(subdiag)
            krylov_basis = krylov_basis.at[column + 1].set(remainder / subdiag)
    coefficients = exponent_column(hessenberg)
    entries = float(length * lax.axis_size("group") * sector_count)
    rescale = jnp.sqrt(jnp.float32(entries)) / jnp.sqrt(jnp.sum(coefficients * coefficients))
    evolved = jnp.dot(coefficients, krylov_basis, precision=HIGH) * rescale
    return (evolved.reshape(state.shape), hessenberg)


def solution(mesh):
    return jax.shard_map(
        local,
        mesh=mesh,
        in_specs=(
            P(("group", "sector"), None, None, None),
            P("group", None, None),
            P(("group", "sector"), None, None, None),
            P(("group", "sector"), None, None, None),
            P(("group", "sector")),
            P(("group", "sector")),
            P(("group", "sector"), None),
        ),
        out_specs=(P(("group", "sector"), None, None, None), P()),
        check_vma=False,
    )
```

profile of v0, /device:TPU:1, one launch (start us, length us, event | category | flops | bytes accessed | tf_op | source)
XLA Modules:
  0.0 1426.7 jit_solution(5528872670102120557)
XLA Ops:
  0.6 3.2 copy.268
  4.3 22.4 %reduce.92 = bf16[4096,128]{1,0:T(8,128)(2,1)S(1)} reduce(bf16[4096,1,128]{2,1,0:T(2,128)(2,1)S(1)} %bitcast.420, bf16[]{:T(256)} %broadcast.443), dimensions={1}, to_apply=%bitcast.409.reduce_sub_computation | reduce | bytes 2097154
  27.9 9.6 all-to-all-start
  38.8 3.2 copy.267
  42.0 23.4 %reduce.93 = bf16[4096,128]{1,0:T(8,128)(2,1)} reduce(bf16[4096,1,128]{2,1,0:T(2,128)(2,1)S(1)} %bitcast.421, bf16[]{:T(256)} %broadcast.443), dimensions={1}, to_apply=%bitcast.408.reduce_sub_computation | reduce | bytes 2097154
  69.7 13.4 all-reduce.4
  83.9 8.1 all-to-all-start.2
  95.2 13.8 all-to-all-done.2
  109.0 3.9 all-to-all-start.1
  113.0 11.2 all_gather.9
  124.2 66.7 %psum.112 = f32[]{:T(128)} all-reduce(f32[]{:T(128)} %multiply_reduce_fusion.7), channel_id=1, replica_groups=mesh['group'=4,'sector'=32] {'group','sector'}, use_global_device_ids=true, to_apply=%region_2.3 | all-reduce | flops 1 | bytes 8 | tf_op jit(solution)/shard_map/psum | solution.py:77
  197.0 4.3 reshape.1111
  205.7 5.5 all-to-all-start.3
  214.5 6.9 reshape.960
  221.4 7.6 fusion
  229.0 3.9 fusion.68
  233.8 4.6 fusion.94
  238.5 64.9 %psum.113 = f32[8]{0:T(128)S(1)} all-reduce(f32[8]{0:T(128)S(1)} %fusion.94), channel_id=1, replica_groups=mesh['group'=4,'sector'=32] {'group','sector'}, use_global_device_ids=true, to_apply=%region_3.5 | all-reduce | flops 8 | bytes 64 | tf_op jit(solution)/shard_map/psum | solution.py:88
  306.9 64.2 %psum.114 = f32[]{:T(128)} all-reduce(f32[]{:T(128)} %get-tuple-element.315), channel_id=1, replica_groups=mesh['group'=4,'sector'=32] {'group','sector'}, use_global_device_ids=true, to_apply=%region_5.7 | all-reduce | flops 1 | bytes 8 | tf_op jit(solution)/shard_map/psum | solution.py:91
  375.8 7.0 reshape.967
  382.8 5.7 fusion.1
  390.0 4.2 scatter.81
  394.2 4.6 convolution_bitcast_fusion.6
  398.8 62.7 %psum.115 = f32[8]{0:T(128)S(1)} all-reduce(f32[8]{0:T(128)S(1)} %convolution_bitcast_fusion.6), channel_id=1, replica_groups=mesh['group'=4,'sector'=32] {'group','sector'}, use_global_device_ids=true, to_apply=%region_7.9 | all-reduce | flops 8 | bytes 64 | tf_op jit(solution)/shard_map/psum | solution.py:88
  464.7 64.0 %psum.116 = f32[]{:T(128)} all-reduce(f32[]{:T(128)} %get-tuple-element.311), channel_id=1, replica_groups=mesh['group'=4,'sector'=32] {'group','sector'}, use_global_device_ids=true, to_apply=%region_9.11 | all-reduce | flops 1 | bytes 8 | tf_op jit(solution)/shard_map/psum | solution.py:91
  531.3 3.2 convolution_convert_fusion.5
  534.4 6.9 reshape.972
  541.4 5.7 fusion.2
  548.6 4.2 scatter.86
  552.7 4.6 convolution_bitcast_fusion.5
  557.4 62.9 %psum.117 = f32[8]{0:T(128)S(1)} all-reduce(f32[8]{0:T(128)S(1)} %convolution_bitcast_fusion.5), channel_id=1, replica_groups=mesh['group'=4,'sector'=32] {'group','sector'}, use_global_device_ids=true, to_apply=%region_11.13 | all-reduce | flops 8 | bytes 64 | tf_op jit(solution)/shard_map/psum | solution.py:88
  623.5 64.1 %psum.118 = f32[]{:T(128)} all-reduce(f32[]{:T(128)} %get-tuple-element.307), channel_id=1, replica_groups=mesh['group'=4,'sector'=32] {'group','sector'}, use_global_device_ids=true, to_apply=%region_13.15 | all-reduce | flops 1 | bytes 8 | tf_op jit(solution)/shard_map/psum | solution.py:91
  689.9 3.2 convolution_convert_fusion.4
  693.1 6.9 reshape.977
  700.0 5.7 fusion.3
  707.2 4.2 scatter.91
  711.4 4.6 convolution_bitcast_fusion.4
  716.0 62.7 %psum.119 = f32[8]{0:T(128)S(1)} all-reduce(f32[8]{0:T(128)S(1)} %convolution_bitcast_fusion.4), channel_id=1, replica_groups=mesh['group'=4,'sector'=32] {'group','sector'}, use_global_device_ids=true, to_apply=%region_15.17 | all-reduce | flops 8 | bytes 64 | tf_op jit(solution)/shard_map/psum | solution.py:88
  781.9 64.1 %psum.120 = f32[]{:T(128)} all-reduce(f32[]{:T(128)} %get-tuple-element.303), channel_id=1, replica_groups=mesh['group'=4,'sector'=32] {'group','sector'}, use_global_device_ids=true, to_apply=%region_17.19 | all-reduce | flops 1 | bytes 8 | tf_op jit(solution)/shard_map/psum | solution.py:91
  848.4 3.2 convolution_convert_fusion.3
  851.5 6.9 reshape.982
  858.5 5.7 fusion.4
  865.7 4.2 scatter.96
  869.8 5.1 convolution_bitcast_fusion.3
  875.0 62.9 %psum.121 = f32[8]{0:T(128)S(1)} all-reduce(f32[8]{0:T(128)} %convolution_bitcast_fusion.3), channel_id=1, replica_groups=mesh['group'=4,'sector'=32] {'group','sector'}, use_global_device_ids=true, to_apply=%region_19.21 | all-reduce | flops 8 | bytes 64 | tf_op jit(solution)/shard_map/psum | solution.py:88
  941.1 64.1 %psum.122 = f32[]{:T(128)} all-reduce(f32[]{:T(128)} %get-tuple-element.299), channel_id=1, replica_groups=mesh['group'=4,'sector'=32] {'group','sector'}, use_global_device_ids=true, to_apply=%region_21.23 | all-reduce | flops 1 | bytes 8 | tf_op jit(solution)/shard_map/psum | solution.py:91
  1007.6 3.2 convolution_convert_fusion.2
  1010.8 6.9 reshape.987
  1017.7 5.7 fusion.5
  1024.9 4.2 scatter.101
  1029.1 5.1 convolution_bitcast_fusion.2
  1034.2 62.7 %psum.123 = f32[8]{0:T(128)} all-reduce(f32[8]{0:T(128)} %convolution_bitcast_fusion.2), channel_id=1, replica_groups=mesh['group'=4,'sector'=32] {'group','sector'}, use_global_device_ids=true, to_apply=%region_23.25 | all-reduce | flops 8 | bytes 64 | tf_op jit(solution)/shard_map/psum | solution.py:88
  1100.8 64.1 %psum.124 = f32[]{:T(128)} all-reduce(f32[]{:T(128)} %get-tuple-element.295), channel_id=1, replica_groups=mesh['group'=4,'sector'=32] {'group','sector'}, use_global_device_ids=true, to_apply=%region_25.27 | all-reduce | flops 1 | bytes 8 | tf_op jit(solution)/shard_map/psum | solution.py:91
  1170.4 6.9 reshape.992
  1177.3 5.7 fusion.6
  1184.6 4.2 scatter.106
  1188.8 4.6 convolution_bitcast_fusion.1
  1193.4 62.7 %psum.125 = f32[8]{0:T(128)S(1)} all-reduce(f32[8]{0:T(128)S(1)} %convolution_bitcast_fusion.1), channel_id=1, replica_groups=mesh['group'=4,'sector'=32] {'group','sector'}, use_global_device_ids=true, to_apply=%region_27.29 | all-reduce | flops 8 | bytes 64 | tf_op jit(solution)/shard_map/psum | solution.py:88
  1259.3 64.1 %psum.126 = f32[]{:T(128)} all-reduce(f32[]{:T(128)} %get-tuple-element.291), channel_id=1, replica_groups=mesh['group'=4,'sector'=32] {'group','sector'}, use_global_device_ids=true, to_apply=%region_29.31 | all-reduce | flops 1 | bytes 8 | tf_op jit(solution)/shard_map/psum | solution.py:91
  1327.8 3.2 convolution_convert_fusion
  1331.0 7.0 reshape.997
  1338.0 5.7 fusion.7
  1347.1 4.6 convolution_bitcast_fusion
  1351.8 62.6 %psum.127 = f32[8,1]{0,1:T(1,128)S(1)} all-reduce(f32[8,1]{0,1:T(1,128)S(1)} %convolution_bitcast_fusion), channel_id=1, replica_groups=mesh['group'=4,'sector'=32] {'group','sector'}, use_global_device_ids=true, to_apply=%region_30.32 | all-reduce | flops 8 | bytes 64 | tf_op jit(solution)/shard_map/psum | solution.py:88
  (171 shorter events, 90.4 us)
Async XLA Ops:
  27.9 56.0 %all-to-all-start = ((bf16[32,2,8192]{2,1,0:T(2,128)(2,1)}), bf16[32,2,8192]{2,1,0:T(2,128)(2,1)S(1)}, u32[]{:S(2)}, u32[]{:S(2)}) async-start(bf16[32,2,8192]{2,1,0:T(2,128)(2,1)} %reshape.1108), calls=%async_computation | async-start | bytes 2097152 | tf_op jit(solution)/shard_map/all_to_all | solution.py:65
  38.8 28.8 %copy-start.22 = (u32[128]{0:T(128)S(1)}, u32[128]{0:T(128)}, u32[]{:S(2)}) copy-start(u32[128]{0:T(128)} %constant.676) | copy-start | bytes 1540
  38.8 44.4 %copy-start.8 = (f32[1,128,4,128]{3,2,1,0:T(4,128)S(1)}, f32[1,128,4,128]{3,2,1,0:T(4,128)}, u32[]{:S(2)}) copy-start(f32[1,128,4,128]{3,2,1,0:T(4,128)} %param.55) | copy-start | bytes 786436
  42.0 50.0 %copy-start.19 = (s32[1,4]{1,0:T(1,128)S(1)}, s32[1,4]{1,0:T(1,128)}, u32[]{:S(2)}) copy-start(s32[1,4]{1,0:T(1,128)} %param.61) | copy-start | bytes 52
  83.9 25.1 %all-to-all-start.2 = ((bf16[32,2,8192]{2,1,0:T(2,128)(2,1)}), bf16[32,2,8192]{2,1,0:T(2,128)(2,1)}, u32[]{:S(2)}, u32[]{:S(2)}) async-start(bf16[32,2,8192]{2,1,0:T(2,128)(2,1)} %reshape.1110), calls=%async_computation.2 | async-start | bytes 2097152 | tf_op jit(solution)/shard_map/all_to_all | solution.py:66
  93.1 19.8 %copy-start.11 = (bf16[8,32,256]{2,1,0:T(8,128)(2,1)S(1)}, bf16[8,32,256]{2,1,0:T(8,128)(2,1)}, u32[]{:S(2)}) copy-start(bf16[8,32,256]{2,1,0:T(8,128)(2,1)} %param.56) | copy-start | bytes 393220
  109.0 96.7 %all-to-all-start.1 = ((bf16[1,32,128,128]{3,2,0,1:T(8,128)(2,1)}), bf16[1,32,128,128]{3,2,0,1:T(8,128)(2,1)S(1)}, u32[]{:S(2)}, u32[]{:S(2)}) async-start(bf16[1,32,128,128]{3,2,0,1:T(8,128)(2,1)} %fusion.106), calls=%async_computation.1 | async-start | bytes 2097152 | tf_op jit(solution)/shard_map/all_to_all | solution.py:70
  192.2 29.2 %copy-start.12 = (bf16[32,4,32,4,1]{0,2,1,4,3:T(8,128)(2,1)}, bf16[32,4,32,4,1]{0,2,1,4,3:T(8,128)(2,1)S(1)}, u32[]{:S(2)}) copy-start(bf16[32,4,32,4,1]{0,2,1,4,3:T(8,128)(2,1)S(1)} %copy.138) | copy-start | bytes 98308
  202.5 8.8 copy-start.9
  205.7 23.3 %all-to-all-start.3 = ((bf16[1,32,128,128]{3,2,0,1:T(8,128)(2,1)}), bf16[1,32,128,128]{3,2,0,1:T(8,128)(2,1)S(1)}, u32[]{:S(2)}, u32[]{:S(2)}) async-start(bf16[1,32,128,128]{3,2,0,1:T(8,128)(2,1)} %fusion.105), calls=%async_computation.3 | async-start | bytes 2097152 | tf_op jit(solution)/shard_map/all_to_all | solution.py:71
  229.0 4.1 copy-start
  233.0 0.7 copy-start.10
  303.5 68.4 %copy-start.20 = (f32[8]{0:T(128)}, f32[8]{0:T(128)S(1)}, u32[]{:S(2)}) copy-start(f32[8]{0:T(128)S(1)} %psum.113) | copy-start | bytes 100
  375.8 7.0 copy-start.13
  382.8 5.7 copy-start.1
  541.4 5.7 copy-start.2
  700.0 5.7 copy-start.3
  858.5 5.7 copy-start.4
  1017.7 5.7 copy-start.5
  1177.3 5.7 copy-start.6
  1184.4 139.6 %copy-start.21 = (f32[8]{0:T(128)S(1)}, f32[8]{0:T(128)}, u32[]{:S(2)}) copy-start(f32[8]{0:T(128)} %copy-done.20) | copy-start | bytes 100
  1256.1 70.7 %copy-start.16 = (f32[8]{0:T(128)}, f32[8]{0:T(128)S(1)}, u32[]{:S(2)}) copy-start(f32[8]{0:T(128)S(1)} %psum.125) | copy-start | bytes 100
  1331.0 7.0 copy-start.14
  1338.0 5.7 copy-start.7
  1343.7 8.0 copy-start.18
  1343.7 74.2 %copy-start.15 = (f32[8]{0:T(128)S(1)}, f32[8]{0:T(128)}, u32[]{:S(2)}) copy-start(f32[8]{0:T(128)} %psum.123) | copy-start | bytes 100
  1343.8 75.0 %copy-start.17 = (f32[8]{0:T(128)S(1)}, f32[8]{0:T(128)}, u32[]{:S(2)}) copy-start(f32[8]{0:T(128)} %copy-done.16) | copy-start | bytes 100
where the time goes:
time: 1440 us; the launch traced here: 1430 us
  blocking collectives  1040 us (72%)
  matrix products  142 us (10%)
  local copies, waits for them, and re-layouts  110 us (8%)
  other arithmetic  81.1 us (6%)
  starting transfers between devices  27.1 us (2%)
    psum x8, blocking collectives, local(): projection = lax.psum(local_projection, ('group', 'sector'))  504 us
    psum x7, blocking collectives, local(): norm_sq = lax.psum(jnp.sum(remainder * remainder), ('group', 'sector'))  449 us
    psum x1, blocking collectives, local(): start_sq = lax.psum(jnp.sum(flattened * flattened), ('group', 'sector'))  66.7 us
    another operation x9, local copies, waits for them, and re-layouts  55.6 us
    dot_general x8, matrix products, apply_sector(): jnp.einsum('aiqj,aqcp->cipj', inner, mixing, preferred_element_type=jnp.f...  47.6 us
    unnamed x2, other arithmetic  45.8 us
    dot_general x8, matrix products, local(): local_projection = jnp.dot(krylov_basis, applied, precision=HIGH)  38 us
  transfers between devices with their start and end apart: 4, of which 1 were waited for; matrix products, arithmetic and copies ran while one was open for 5% of the time, Pallas kernels for 0%

commit v1 on v0

v1 whole, which is shorter than its diff:
```python
import functools

import jax
import jax.numpy as jnp
from jax import lax
from jax.experimental import pallas as pl
from jax.experimental.pallas import tpu as pltpu
from jax.sharding import PartitionSpec as P

MESH = pl.DeviceIdType.MESH
HIGH = lax.Precision.HIGHEST
F32 = jnp.float32
BF16 = jnp.bfloat16

KRYLOV = 8
TAU = 3.0
EPS = 1e-06
VMEM_LIMIT = 56 * 1024 * 1024


def route_kernel(
    lm_ref, rm_ref, panel_ref, left_ref, right_ref,
    left_out, right_out, panel_out,
    spread_l, spread_r, stage_l, stage_r, turned, match_v, match_s,
    send_l, recv_l, send_r, recv_r, send_l2, recv_l2, send_r2, recv_r2,
    send_m, recv_m, send_p, recv_p, own_sem,
):
    group = lax.axis_index("group")
    me = lax.axis_index("sector")
    groups = lax.axis_size("group")
    n = lax.axis_size("sector")

    barrier = pltpu.get_barrier_semaphore()

    def greet(k, _):
        pl.semaphore_signal(barrier, inc=1, device_id=(group, lax.rem(me + k, n)), device_id_type=MESH)
        return 0

    lax.fori_loop(1, n, greet, 0)
    for k in range(1, groups):
        pl.semaphore_signal(barrier, inc=1, device_id=(lax.rem(group + k, groups), me), device_id_type=MESH)

    lane = lax.broadcasted_iota(jnp.int32, (1, 128), 1)
    match_v[me] = jnp.where(lane == 0, lm_ref[0], rm_ref[0])
    own = [
        pltpu.make_async_copy(left_ref.at[me], spread_l.at[me], own_sem.at[0]),
        pltpu.make_async_copy(panel_ref, panel_out.at[group], own_sem.at[1]),
    ]
    for copy in own:
        copy.start()
    pl.semaphore_wait(barrier, n - 1 + groups - 1)

    def remote(src, dst, send, recv, peer):
        return pltpu.make_async_remote_copy(
            src_ref=src, dst_ref=dst, send_sem=send, recv_sem=recv, device_id=(group, peer), device_id_type=MESH
        )

    def spread_left(peer, slot):
        return remote(left_ref.at[peer], spread_l.at[slot], send_l.at[peer], recv_l.at[slot], peer)

    def spread_right(peer, slot):
        return remote(turned.at[peer], spread_r.at[slot], send_r.at[peer], recv_r.at[slot], peer)

    def tell(peer, slot):
        return remote(match_v.at[slot], match_v.at[slot], send_m.at[peer], recv_m.at[slot], peer)

    def route_left(peer, slot):
        return remote(stage_l.at[peer], left_out.at[slot], send_l2.at[peer], recv_l2.at[slot], peer)

    def route_right(peer, slot):
        return remote(stage_r.at[peer], right_out.at[slot], send_r2.at[peer], recv_r2.at[slot], peer)

    def panel_copy(k, slot):
        other = lax.rem(group + k, groups)
        return pltpu.make_async_remote_copy(
            src_ref=panel_ref, dst_ref=panel_out.at[slot], send_sem=send_p.at[other], recv_sem=recv_p.at[slot],
            device_id=(other, me), device_id_type=MESH,
        )

    def each_peer(body):
        def step(k, _):
            body(lax.rem(me + k, n))
            return 0

        lax.fori_loop(1, n, step, 0)

    def start_left(peer):
        tell(peer, me).start()
        spread_left(peer, me).start()

    each_peer(start_left)
    for k in range(1, groups):
        panel_copy(k, group).start()

    def turn(k, _):
        peer = lax.rem(me + k, n)
        turned[peer] = right_ref[peer].astype(F32).T.astype(BF16)

        @pl.when(k < n)
        def _():
            spread_right(peer, me).start()

        return 0

    lax.fori_loop(1, n + 1, turn, 0)
    spread_r[me] = turned[me]

    each_peer(lambda peer: tell(peer, peer).wait_recv())
    to_scalar = pltpu.make_async_copy(match_v, match_s, own_sem.at[2])
    to_scalar.start()
    own[0].wait()
    to_scalar.wait()
    each_peer(lambda peer: spread_left(peer, peer).wait_recv())

    def pick_left(peer):
        stage_l[peer] = spread_l[match_s[peer, 0, 0]]
        route_left(peer, me).start()

    each_peer(pick_left)
    stage_l[me] = spread_l[match_s[me, 0, 0]]
    keep_l = pltpu.make_async_copy(stage_l.at[me], left_out.at[me], own_sem.at[0])
    keep_l.start()

    each_peer(lambda peer: spread_right(peer, peer).wait_recv())

    def pick_right(peer):
        stage_r[peer] = spread_r[match_s[peer, 0, 1]]
        route_right(peer, me).start()

    each_peer(pick_right)
    stage_r[me] = spread_r[match_s[me, 0, 1]]
    keep_r = pltpu.make_async_copy(stage_r.at[me], right_out.at[me], own_sem.at[2])
    keep_r.start()

    own[1].wait()
    for k in range(1, groups):
        other = lax.rem(group + k, groups)
        panel_copy(k, other).wait_recv()
        panel_copy(k, group).wait_send()

    def finish(peer):
        tell(peer, me).wait_send()
        spread_left(peer, me).wait_send()
        spread_right(peer, me).wait_send()
        route_left(peer, me).wait_send()
        route_right(peer, me).wait_send()

    each_peer(finish)
    keep_l.wait()
    keep_r.wait()

    def arrived(peer):
        route_left(peer, peer).wait_recv()
        route_right(peer, peer).wait_recv()

    each_peer(arrived)


def route(left_match, right_match, panel, left_env, right_env, n, groups):
    channels, block = left_env.shape[1], left_env.shape[2]
    piece = (n, block, block)
    sems = [pltpu.SemaphoreType.DMA((n,))] * 10
    return pl.pallas_call(
        route_kernel,
        out_shape=(
            jax.ShapeDtypeStruct((channels, block, block), BF16),
            jax.ShapeDtypeStruct((channels, block, block), BF16),
            jax.ShapeDtypeStruct((groups,) + panel.shape, BF16),
        ),
        in_specs=[
            pl.BlockSpec(memory_space=pltpu.SMEM),
            pl.BlockSpec(memory_space=pltpu.SMEM),
            pl.BlockSpec(memory_space=pltpu.VMEM),
            pl.BlockSpec(memory_space=pltpu.VMEM),
            pl.BlockSpec(memory_space=pltpu.VMEM),
        ],
        out_specs=(
            pl.BlockSpec(memory_space=pltpu.VMEM),
            pl.BlockSpec(memory_space=pltpu.VMEM),
            pl.BlockSpec(memory_space=pltpu.VMEM),
        ),
        scratch_shapes=[pltpu.VMEM(piece, BF16)] * 5
        + [pltpu.VMEM((n, 1, 128), jnp.int32), pltpu.SMEM((n, 1, 128), jnp.int32)]
        + sems
        + [pltpu.SemaphoreType.DMA((groups,))] * 2
        + [pltpu.SemaphoreType.DMA((3,))],
        compiler_params=pltpu.CompilerParams(
            collective_id=0, has_side_effects=True, vmem_limit_bytes=VMEM_LIMIT
        ),
        name="route",
    )(left_match, right_match, panel, left_env[0], right_env[0])


def total(value):
    return jnp.sum(jnp.sum(value, axis=0, keepdims=True), axis=1, keepdims=True)


def fold(value):
    rows, columns = value.shape
    out = jnp.sum(value.reshape(rows // 8, 8, columns), axis=0)
    acc = out[:, :128]
    for start in range(128, columns, 128):
        acc = acc + out[:, start : start + 128]
    return acc


def sector_kernel(states_ref, state_ref, panel_ref, left_ref, right_ref, basis_ref, row_ref, chosen, spread, rt32, joint, z, x, y):
    channels, block = left_ref.shape[0], left_ref.shape[1]
    phys = states_ref.shape[1]
    wide = phys * block
    lane = lax.broadcasted_iota(jnp.int32, (1, 128), 1)

    pick = lax.broadcasted_iota(jnp.int32, (16, 256), 0)
    want = jnp.zeros((16, 256), jnp.int32)
    for p in range(phys):
        for q in range(phys):
            want = jnp.where(pick == p * phys + q, 16 * states_ref[0, q] + states_ref[0, p], want)
    choose = (want == lax.broadcasted_iota(jnp.int32, (16, 256), 1)).astype(BF16)
    chosen[...] = lax.dot_general(
        choose, panel_ref[...], (((1,), (1,)), ((), ())), preferred_element_type=F32
    )

    grow = (
        lax.broadcasted_iota(jnp.int32, (channels, 8 * channels), 0)
        == lax.broadcasted_iota(jnp.int32, (channels, 8 * channels), 1) // 8
    ).astype(BF16)
    same = lax.broadcasted_iota(jnp.int32, (1, 8, 8 * channels), 1) == lax.rem(
        lax.broadcasted_iota(jnp.int32, (1, 8, 8 * channels), 2), 8
    )
    for p in range(phys):
        rows = jnp.concatenate(
            [chosen[p * phys : (p + 1) * phys, a * channels : (a + 1) * channels] for a in range(channels)], axis=0
        )
        grown = jnp.dot(rows.astype(BF16), grow, preferred_element_type=F32)
        spread[p] = (
            jnp.where(same, grown[:, None, :], 0.0).reshape(channels * phys * 8, 8 * channels).astype(BF16)
        )

    def widen(c, _):
        rt32[c] = right_ref[c].astype(F32)
        return 0

    lax.fori_loop(0, channels, widen, 0)

    def join(m, _):
        start = pl.multiple_of(m * 16, 16)
        upper = rt32[:, pl.ds(start, 8), :].reshape(channels * 8, block)
        lower = rt32[:, pl.ds(start + 8, 8), :].reshape(channels * 8, block)
        both = jnp.concatenate([upper, lower], axis=1).astype(BF16)
        for p in range(phys):
            out = jnp.dot(spread[p], both, preferred_element_type=F32)
            tiles = out.reshape(channels * phys, 8, 2 * block)
            joint[:, pl.ds(start, 16), p * block : (p + 1) * block] = jnp.concatenate(
                [tiles[:, :, :block], tiles[:, :, block:]], axis=1
            ).astype(BF16)
        return 0

    lax.fori_loop(0, block // 16, join, 0)

    big = jnp.max(jnp.max(jnp.abs(state_ref[...]), axis=0, keepdims=True), axis=1, keepdims=True)
    shrink = jnp.where(big > 0.0, 1.0 / big, 0.0)
    for q in range(phys):
        part = state_ref[pl.ds(q, block, stride=phys), :] * shrink
        basis_ref[0, :, q * block : (q + 1) * block] = part
    size = jnp.sqrt(total(fold(basis_ref[0] * basis_ref[0])))
    first = basis_ref[0] * jnp.where(size > 0.0, 1.0 / size, 0.0)
    basis_ref[0] = first
    x[...] = first.astype(BF16)
    for j in range(1, KRYLOV):
        basis_ref[j] = jnp.zeros((block, wide), F32)
    row = jnp.where(lane == 64, big * size, 0.0)

    def apply():
        def left(a, _):
            z[a] = jnp.dot(left_ref[a], x[...], preferred_element_type=F32).astype(BF16)
            return 0

        lax.fori_loop(0, channels, left, 0, unroll=4)
        y[...] = jnp.zeros_like(y)

        def right(a, _):
            weights = joint[pl.ds(pl.multiple_of(a * phys, phys), phys)].reshape(phys * block, wide)
            y[...] += jnp.dot(z[a], weights, preferred_element_type=F32)
            return 0

        lax.fori_loop(0, channels, right, 0, unroll=4)

    for t in range(KRYLOV):
        apply()
        applied = y[...]
        heights = [total(fold(basis_ref[j] * applied)) for j in range(t + 1)]
        for j in range(t + 1):
            row = jnp.where(lane == t * KRYLOV + j, heights[j], row)
        if t + 1 < KRYLOV:
            rest = applied
            for j in range(t + 1):
                rest = rest - heights[j] * basis_ref[j]
            square = total(fold(rest * rest))
            scale = jnp.where(square > 0.0, lax.rsqrt(square), 0.0)
            new = rest * scale
            basis_ref[t + 1] = new
            x[...] = new.astype(BF16)
            row = jnp.where(lane == t * KRYLOV + t + 1, square * scale, row)
    row_ref[...] = row


def sector(states, state, panel, left, right):
    channels, block = left.shape[0], left.shape[1]
    phys = states.shape[1]
    wide = phys * block
    vmem = pl.BlockSpec(memory_space=pltpu.VMEM)
    return pl.pallas_call(
        sector_kernel,
        out_shape=(
            jax.ShapeDtypeStruct((KRYLOV, block, wide), F32),
            jax.ShapeDtypeStruct((1, 128), F32),
        ),
        in_specs=[pl.BlockSpec(memory_space=pltpu.SMEM), vmem, vmem, vmem, vmem],
        out_specs=(vmem, vmem),
        scratch_shapes=[
            pltpu.VMEM((phys * phys, channels * channels), F32),
            pltpu.VMEM((phys, channels * phys * 8, channels * 8), BF16),
            pltpu.VMEM((channels, block, block), F32),
            pltpu.VMEM((channels * phys, block, wide), BF16),
            pltpu.VMEM((channels, block, wide), BF16),
            pltpu.VMEM((block, wide), BF16),
            pltpu.VMEM((block, wide), F32),
        ],
        compiler_params=pltpu.CompilerParams(vmem_limit_bytes=VMEM_LIMIT),
        name="sector",
    )(states, state, panel, left, right)


def multiply(a, b):
    out = a[:, 0:1] * b[0:1, :]
    for k in range(1, KRYLOV):
        out = out + a[:, k : k + 1] * b[k : k + 1, :]
    return out


def joint_kernel(row_ref, hess_ref, weight_ref, table, send_a, recv_a, send_b, recv_b):
    group = lax.axis_index("group")
    me = lax.axis_index("sector")
    groups = lax.axis_size("group")
    n = lax.axis_size("sector")
    near = 8
    lines = n // near
    line, place = me // near, lax.rem(me, near)
    home = group * lines + line

    def next_near(k):
        return (group, line * near + lax.rem(place + k, near))

    def next_far(k):
        other = lax.rem(home + k, groups * lines)
        return (other // lines, lax.rem(other, lines) * near + place)

    barrier = pltpu.get_barrier_semaphore()
    for k in range(1, near):
        pl.semaphore_signal(barrier, inc=1, device_id=next_near(k), device_id_type=MESH)
    for k in range(1, groups * lines):
        pl.semaphore_signal(barrier, inc=1, device_id=next_far(k), device_id_type=MESH)
    table[home, pl.ds(place, 1), :] = row_ref[...]
    pl.semaphore_wait(barrier, near - 1 + groups * lines - 1)

    def near_copy(k, slot):
        piece = table.at[home, pl.ds(slot, 1), :]
        return pltpu.make_async_remote_copy(
            src_ref=piece, dst_ref=piece, send_sem=send_a.at[k], recv_sem=recv_a.at[slot],
            device_id=next_near(k), device_id_type=MESH,
        )

    def far_copy(k, slot):
        piece = table.at[slot]
        return pltpu.make_async_remote_copy(
            src_ref=piece, dst_ref=piece, send_sem=send_b.at[k], recv_sem=recv_b.at[slot],
            device_id=next_far(k), device_id_type=MESH,
        )

    for k in range(1, near):
        near_copy(k, place).start()
    for k in range(1, near):
        near_copy(k, lax.rem(place + k, near)).wait_recv()
    for k in range(1, groups * lines):
        far_copy(k, home).start()
    for k in range(1, groups * lines):
        far_copy(k, lax.rem(home + k, groups * lines)).wait_recv()

    entries = table[...].reshape(groups * n, 128).T
    columns = [entries[t * KRYLOV : (t + 1) * KRYLOV, :] for t in range(KRYLOV)]
    norms = entries[64:65, :]
    sub = lax.broadcasted_iota(jnp.int32, (KRYLOV, 128), 0)
    lane = lax.broadcasted_iota(jnp.int32, (KRYLOV, 128), 1)

    start_sq = total(norms * norms)
    vectors = [jnp.where(sub == 0, norms / jnp.sqrt(start_sq + EPS), 0.0)]
    hess = jnp.zeros((KRYLOV, 128), F32)
    for t in range(KRYLOV):
        now = vectors[t]
        applied = columns[0] * now[0:1, :]
        for i in range(1, t + 1):
            applied = applied + columns[i] * now[i : i + 1, :]
        heights = [total(vectors[j] * applied) for j in range(t + 1)]
        for j in range(t + 1):
            hess = jnp.where((sub == j) & (lane == t), heights[j], hess)
        if t + 1 < KRYLOV:
            rest = applied
            for j in range(t + 1):
                rest = rest - heights[j] * vectors[j]
            beta = jnp.sqrt(total(rest * rest) + EPS)
            hess = jnp.where((sub == t + 1) & (lane == t), beta, hess)
            vectors.append(rest / beta)

    scaled = (-TAU / 16.0) * hess
    power = jnp.where(sub == lane, 1.0, 0.0).astype(F32)
    series = power
    for order in range(1, 11):
        power = multiply(power, scaled) / float(order)
        series = series + power
    for _ in range(4):
        series = multiply(series, series)
    coefficients = series[:, 0:1]
    entries_total = float(groups * n * 128 * 4 * 128)
    rescale = jnp.sqrt(jnp.full((1, 1), entries_total, F32)) / jnp.sqrt(
        jnp.sum(coefficients * coefficients, axis=0, keepdims=True)
    )
    mixed = coefficients[0:1, :] * vectors[0]
    for t in range(1, KRYLOV):
        mixed = mixed + coefficients[t : t + 1, :] * vectors[t]
    mine = jnp.sum(jnp.where(lane == group * n + me, mixed, 0.0), axis=1, keepdims=True)
    hess_ref[...] = hess[:, :KRYLOV]
    weight_ref[...] = jnp.broadcast_to(mine * rescale, (KRYLOV, 128))

    for k in range(1, near):
        near_copy(k, place).wait_send()
    for k in range(1, groups * lines):
        far_copy(k, home).wait_send()


def join_sectors(row, n, groups):
    vmem = pl.BlockSpec(memory_space=pltpu.VMEM)
    lines = n // 8
    return pl.pallas_call(
        joint_kernel,
        out_shape=(
            jax.ShapeDtypeStruct((KRYLOV, KRYLOV), F32),
            jax.ShapeDtypeStruct((KRYLOV, 128), F32),
        ),
        in_specs=[vmem],
        out_specs=(vmem, vmem),
        scratch_shapes=[
            pltpu.VMEM((groups * lines, 8, 128), F32),
            pltpu.SemaphoreType.DMA((8,)),
            pltpu.SemaphoreType.DMA((8,)),
            pltpu.SemaphoreType.DMA((groups * lines,)),
            pltpu.SemaphoreType.DMA((groups * lines,)),
        ],
        compiler_params=pltpu.CompilerParams(collective_id=1, has_side_effects=True),
        name="joint",
    )(row)


def evolve_kernel(basis_ref, weight_ref, out_ref):
    phys = basis_ref.shape[2] // 128
    block = basis_ref.shape[1]
    for p in range(phys):
        acc = weight_ref[0:1, :] * basis_ref[0, :, p * 128 : (p + 1) * 128]
        for j in range(1, KRYLOV):
            acc = acc + weight_ref[j : j + 1, :] * basis_ref[j, :, p * 128 : (p + 1) * 128]
        out_ref[pl.ds(p, block, stride=phys), :] = acc


def evolve(basis, weight):
    vmem = pl.BlockSpec(memory_space=pltpu.VMEM)
    block, wide = basis.shape[1], basis.shape[2]
    return pl.pallas_call(
        evolve_kernel,
        out_shape=jax.ShapeDtypeStruct((block * wide // 128, 128), F32),
        in_specs=[vmem, vmem],
        out_specs=vmem,
        compiler_params=pltpu.CompilerParams(vmem_limit_bytes=VMEM_LIMIT),
        name="evolve",
    )(basis, weight)


def local(state, panel, left_env, right_env, left_match, right_match, phys_states):
    n, groups = lax.axis_size("sector"), lax.axis_size("group")
    left, right, full_panel = route(left_match, right_match, panel, left_env, right_env, n, groups)
    channels = left.shape[0]
    flat_panel = full_panel.reshape(channels * full_panel.shape[2], full_panel.shape[3])
    rows = state.reshape(-1, state.shape[-1])
    basis, row = sector(phys_states, rows, flat_panel, left, right)
    hess, weight = join_sectors(row, n, groups)
    return evolve(basis, weight).reshape(state.shape), hess


def solution(mesh):
    return jax.shard_map(
        local,
        mesh=mesh,
        in_specs=(
            P(("group", "sector"), None, None, None),
            P("group", None, None),
            P(("group", "sector"), None, None, None),
            P(("group", "sector"), None, None, None),
            P(("group", "sector")),
            P(("group", "sector")),
            P(("group", "sector"), None),
        ),
        out_specs=(P(("group", "sector"), None, None, None), P()),
        check_vma=False,
    )
```

time: 1440 us -> 150 us (0.10)
  blocking collectives: 1040 us -> 0 us
  Pallas kernels: 0 us -> 148 us
  matrix products: 142 us -> 0 us
  local copies, waits for them, and re-layouts: 110 us -> 0.6 us
  other arithmetic: 81.1 us -> 0 us
  starting transfers between devices: 27.1 us -> 0 us
    psum x16 -> x0, blocking collectives: 1020 us -> none  [the longest x8 504 us: local(): projection = lax.psum(local_projection, ('group', 'sector'))]
    pallas_call x0 -> x4, Pallas kernels: none -> 148 us  [the longest x1 66.7 us: route(): pl.pallas_call(route_kernel, out_shape=(jax.ShapeDtypeStruct((channels, b...]
    dot_general x55 -> x0, matrix products: 142 us -> none  [the longest x8 47.6 us: apply_sector(): jnp.einsum('aiqj,aqcp->cipj', inner, mixing, preferred_element_type=jnp.f...]
    another operation x9 -> x0, local copies, waits for them, and re-layouts: 55.6 us -> none
    unnamed x2 -> x0, other arithmetic: 45.8 us -> none
    scatter x23 -> x0, local copies, waits for them, and re-layouts: 28.4 us -> none  [the longest x7 26.8 us: local(): krylov_basis = krylov_basis.at[column + 1].set(remainder / subdiag)]
    all_to_all x4 -> x0, starting transfers between devices: 27.1 us -> none  [the longest x1 9.6 us: local(): lax.all_to_all(left_rows, 'sector', split_axis=1, concat_axis=0, tiled=True)]
  transfers between devices with their start and end apart: 4 -> 0, of which waited for: 1 -> 0; matrix products, arithmetic and copies ran while one was open for 5% -> 0% of each run, Pallas kernels for 0% -> 0%
where the time goes in v1:
time: 150 us
  Pallas kernels  148 us (99%)
  between operations  1.95 us (1%)
    pallas_call x1, Pallas kernels, route(): pl.pallas_call(route_kernel, out_shape=(jax.ShapeDtypeStruct((channels, b...  66.7 us
    pallas_call x1, Pallas kernels, sector(): pl.pallas_call(sector_kernel, out_shape=(jax.ShapeDtypeStruct((KRYLOV, bl...  59.1 us
    pallas_call x1, Pallas kernels, join_sectors(): pl.pallas_call(joint_kernel, out_shape=(jax.ShapeDtypeStruct((KRYLOV, KRY...  19.2 us

profile of v1, /device:TPU:1, one launch (start us, length us, event | category | flops | bytes accessed | tf_op | source)
XLA Modules:
  0.0 150.1 jit_solution(17804474162209050613)
XLA Ops:
  1.9 66.7 %route.1 = (bf16[32,128,128]{2,1,0:T(8,128)(2,1)}, bf16[32,128,128]{2,1,0:T(8,128)(2,1)}, bf16[4,8,32,256]{3,2,1,0:T(8,128)(2,1)}) custom-call(s32[1]{0:T(128)S(6)} %copy.10.lm_ref, s32[1]{0:T(128)S(6)} %copy.11.rm_ref, bf16[8,32,256]{2,1,0:T(8,128)(2,1)} %panel_ref.1, bf16[32,128,128]{2,1,0:T(8,128)(2,1)} %bitcast.5, bf16[32,128,128]{2,1,0:T(8,128)(2,1)} %bitcast.6), custom_call_target="tpu_custom_call" | custom-call | tf_op jit(solution)/shard_map/route/pallas_call | solution.py:163
  68.6 59.1 %sector.1 = (f32[8,128,512]{2,1,0:T(8,128)}, f32[1,128]{1,0:T(1,128)}) custom-call(s32[1,4]{1,0:T(1,128)} %states_ref.1, f32[512,128]{1,0:T(8,128)} %bitcast.8, bf16[1024,256]{1,0:T(8,128)(2,1)} %bitcast.7, bf16[32,128,128]{2,1,0:T(8,128)(2,1)} %get-tuple-element.10.left_ref, bf16[32,128,128]{2,1,0:T(8,128)(2,1)} %get-tuple-element.11.right_ref), custom_call_target="tpu_custom_call" | custom-call | tf_op jit(solution)/shard_map/sector/pallas_call | solution.py:312
  127.7 19.2 %joint.1 = (f32[8,8]{1,0:T(8,128)}, f32[8,128]{1,0:T(8,128)}) custom-call(f32[1,128]{1,0:T(1,128)} %get-tuple-element.13.row_ref), custom_call_target="tpu_custom_call" | custom-call | tf_op jit(solution)/shard_map/joint/pallas_call | solution.py:443
  146.9 0.0 copy-start
  147.0 2.5 %evolve.1 = f32[512,128]{1,0:T(8,128)} custom-call(f32[8,128,512]{2,1,0:T(8,128)} %get-tuple-element.12.basis_ref, f32[8,128]{1,0:T(8,128)} %get-tuple-element.14.weight_ref), custom_call_target="tpu_custom_call" | custom-call | tf_op jit(solution)/shard_map/evolve/pallas_call | solution.py:476
  149.5 0.0 copy-done
  149.5 0.6 copy.12
Async XLA Ops:
  146.9 2.5 %copy-start = (f32[8,8]{1,0:T(8,128)S(1)}, f32[8,8]{1,0:T(8,128)}, u32[]{:S(2)}) copy-start(f32[8,8]{1,0:T(8,128)} %get-tuple-element.19) | copy-start | bytes 772

commit v2 on v0

v2 whole, which is shorter than its diff:
```python
import functools

import jax
import jax.numpy as jnp
from jax import lax
from jax.experimental import pallas as pl
from jax.experimental.pallas import tpu as pltpu
from jax.sharding import PartitionSpec as P

MESH = pl.DeviceIdType.MESH
F32 = jnp.float32
BF16 = jnp.bfloat16

KRYLOV = 8
TAU = 3.0
EPS = 1e-06
VMEM_LIMIT = 56 * 1024 * 1024
SIDE = 4
HALVES = 2


def far_first():
    def away(offset):
        return min(offset[0], SIDE - offset[0]) + min(offset[1], SIDE - offset[1])

    every = [(y, z, c) for y in range(SIDE) for z in range(SIDE) for c in range(2)]
    order = []
    for offset in sorted(every[1:], key=lambda o: -away(o)):
        for _ in range(4):
            if offset not in order and offset in every[1:]:
                order.append(offset)
            offset = (offset[1], (SIDE - offset[0]) % SIDE, offset[2])
    return order


ORDER = far_first()


def total(value):
    return jnp.sum(jnp.sum(value, axis=0, keepdims=True), axis=1, keepdims=True)


def narrow(value):
    return (value[:, :128] + value[:, 128:256]) + (value[:, 256:384] + value[:, 384:])


def multiply(a, b):
    out = a[:, 0:1] * b[0:1, :]
    for k in range(1, KRYLOV):
        out = out + a[:, k : k + 1] * b[k : k + 1, :]
    return out


def kernel(
    lm_ref, rm_ref, states_ref, state_ref, panel_ref, left_ref, right_ref,
    out_ref, hess_ref,
    right_v, turned, spread_l, spread_r, stage_l, stage_r, left_in, right_in, match_v, match_s, panels,
    chosen, grown, joint, left_w, z, x, y, basis, row_ref, table,
    own_sem, send_m, recv_m, send_l, recv_l, send_r, recv_r, send_l2, recv_l2, send_r2, recv_r2,
    send_p, recv_p, send_a, recv_a, send_b, recv_b, send_c, recv_c,
):
    group = lax.axis_index("group")
    me = lax.axis_index("sector")
    groups = lax.axis_size("group")
    n = lax.axis_size("sector")
    near = 2 * SIDE
    line, place = me // near, lax.rem(me, near)
    chip, core = lax.rem(me // 2, SIDE), lax.rem(me, 2)
    channels, block = left_in.shape[0], left_in.shape[1]
    phys = states_ref.shape[1]
    wide = phys * block

    def at(offset):
        dy, dz, dc = offset
        return lax.rem(line + dy, SIDE) * near + lax.rem(chip + dz, SIDE) * 2 + lax.rem(core + dc, 2)

    def each_peer(body):
        def step(k, _):
            body(lax.rem(me + k, n))
            return 0

        lax.fori_loop(1, n, step, 0)

    barrier = pltpu.get_barrier_semaphore()
    each_peer(lambda peer: pl.semaphore_signal(barrier, inc=1, device_id=(group, peer), device_id_type=MESH))
    for k in range(1, groups):
        pl.semaphore_signal(barrier, inc=1, device_id=(lax.rem(group + k, groups), me), device_id_type=MESH)

    load_r = pltpu.make_async_copy(right_ref, right_v, own_sem.at[0])
    keep_l = pltpu.make_async_copy(left_ref.at[me], spread_l.at[me], own_sem.at[1])
    load_r.start()
    keep_l.start()
    panels[group] = panel_ref[...]
    lane = lax.broadcasted_iota(jnp.int32, (1, 128), 1)
    match_v[me] = jnp.where(lane == 0, lm_ref[0], rm_ref[0])
    pl.semaphore_wait(barrier, n - 1 + groups - 1)

    def remote(src, dst, send, recv, device):
        return pltpu.make_async_remote_copy(
            src_ref=src, dst_ref=dst, send_sem=send, recv_sem=recv, device_id=device, device_id_type=MESH
        )

    def tell(peer, slot):
        return remote(match_v.at[slot], match_v.at[slot], send_m.at[peer], recv_m.at[slot], (group, peer))

    def spread_left(peer, slot):
        return remote(left_ref.at[peer], spread_l.at[slot], send_l.at[peer], recv_l.at[slot], (group, peer))

    def spread_right(peer, slot):
        return remote(turned.at[peer], spread_r.at[slot], send_r.at[peer], recv_r.at[slot], (group, peer))

    def route_left(peer, slot):
        return remote(stage_l.at[peer], left_in.at[slot], send_l2.at[peer], recv_l2.at[slot], (group, peer))

    part = block // HALVES

    def route_right(h, peer, slot):
        rows = pl.ds(h * part, part)
        return remote(
            stage_r.at[peer, rows], right_in.at[slot, rows], send_r2.at[h, peer], recv_r2.at[h, slot], (group, peer)
        )

    def panel_copy(k, slot):
        other = lax.rem(group + k, groups)
        return remote(panels.at[slot], panels.at[slot], send_p.at[other], recv_p.at[slot], (other, me))

    for offset in ORDER:
        tell(at(offset), me).start()
    for offset in ORDER:
        spread_left(at(offset), me).start()
    for k in range(1, groups):
        panel_copy(k, group).start()
    load_r.wait()

    def turn(peer):
        turned[peer] = right_v[peer].astype(F32).T.astype(BF16)

    for offset in ORDER:
        peer = at(offset)
        turn(peer)
        spread_right(peer, me).start()
    spread_r[me] = right_v[me].astype(F32).T.astype(BF16)

    big = jnp.max(jnp.max(jnp.abs(state_ref[...]), axis=0, keepdims=True), axis=1, keepdims=True)
    shrink = jnp.where(big > 0.0, 1.0 / big, 0.0)
    for q in range(phys):
        y[:, q * block : (q + 1) * block] = state_ref[pl.ds(q, block, stride=phys), :] * shrink
    acc = jnp.zeros((8, 128), F32)
    for r in range(0, block, 8):
        piece = y[r : r + 8, :]
        acc = acc + narrow(piece * piece)
    size = jnp.sqrt(total(acc))
    scale = jnp.where(size > 0.0, 1.0 / size, 0.0)
    for r in range(0, block, 16):
        first = y[r : r + 16, :] * scale
        basis[0, r : r + 16, :] = first
        x[r : r + 16, :] = first.astype(BF16)
    row_ref[...] = jnp.where(lane == 64, big * size, 0.0)

    for k in range(1, groups):
        panel_copy(k, lax.rem(group + k, groups)).wait_recv()
    pick = lax.broadcasted_iota(jnp.int32, (16, 256), 0)
    want = jnp.zeros((16, 256), jnp.int32)
    for p in range(phys):
        for q in range(phys):
            want = jnp.where(pick == p * phys + q, 16 * states_ref[0, q] + states_ref[0, p], want)
    choose = (want == lax.broadcasted_iota(jnp.int32, (16, 256), 1)).astype(BF16)
    chosen[...] = lax.dot_general(
        choose,
        panels[...].reshape(channels * channels, 256),
        (((1,), (1,)), ((), ())),
        preferred_element_type=F32,
    )
    grow = (
        lax.broadcasted_iota(jnp.int32, (channels, 8 * channels), 0)
        == lax.broadcasted_iota(jnp.int32, (channels, 8 * channels), 1) // 8
    ).astype(BF16)
    same = lax.broadcasted_iota(jnp.int32, (1, 8, 8 * channels), 1) == lax.rem(
        lax.broadcasted_iota(jnp.int32, (1, 8, 8 * channels), 2), 8
    )
    for p in range(phys):
        rows = jnp.concatenate(
            [chosen[p * phys : (p + 1) * phys, a * channels : (a + 1) * channels] for a in range(channels)], axis=0
        )
        wider = jnp.dot(rows.astype(BF16), grow, preferred_element_type=F32)
        grown[p] = jnp.where(same, wider[:, None, :], 0.0).reshape(channels * phys * 8, 8 * channels).astype(BF16)

    each_peer(lambda peer: tell(peer, peer).wait_recv())
    to_scalar = pltpu.make_async_copy(match_v, match_s, own_sem.at[2])
    to_scalar.start()
    keep_l.wait()
    to_scalar.wait()
    each_peer(lambda peer: spread_left(peer, peer).wait_recv())
    for offset in ORDER:
        peer = at(offset)
        stage_l[peer] = spread_l[match_s[peer, 0, 0]]
        route_left(peer, me).start()
    left_in[me] = spread_l[match_s[me, 0, 0]]

    each_peer(lambda peer: spread_right(peer, peer).wait_recv())
    for h in range(HALVES):
        for offset in ORDER:
            peer = at(offset)
            if h == 0:
                stage_r[peer] = spread_r[match_s[peer, 0, 1]]
            route_right(h, peer, me).start()
    right_in[me] = spread_r[match_s[me, 0, 1]]

    each_peer(lambda peer: route_left(peer, peer).wait_recv())
    for a in range(channels):
        left_w[:, a * block : (a + 1) * block] = left_in[a]

    def join(m, _):
        start = pl.multiple_of(m * 16, 16)
        lines_in = right_in[:, pl.ds(start, 16), :].astype(F32)
        both = jnp.concatenate(
            [lines_in[:, :8].reshape(channels * 8, block), lines_in[:, 8:].reshape(channels * 8, block)], axis=1
        ).astype(BF16)
        for p in range(phys):
            out = jnp.dot(grown[p], both, preferred_element_type=F32)
            tiles = out.reshape(channels * phys, 8, 2 * block)
            joint[:, pl.ds(start, 16), p * block : (p + 1) * block] = jnp.concatenate(
                [tiles[:, :, :block], tiles[:, :, block:]], axis=1
            ).astype(BF16)
        return 0

    for h in range(HALVES):
        each_peer(lambda peer: route_right(h, peer, peer).wait_recv())
        lax.fori_loop(h * part // 16, (h + 1) * part // 16, join, 0)

    def apply():
        for a in range(channels):
            weights = joint[a * phys : (a + 1) * phys].reshape(wide, wide)
            z[a] = jnp.dot(x[...], weights, preferred_element_type=F32).astype(BF16)
        y[...] = jnp.dot(left_w[...], z[...].reshape(channels * block, wide), preferred_element_type=F32)

    def orthogonalize(t):
        accs = [jnp.zeros((8, 128), F32)] * (t + 1)
        for r in range(0, block, 8):
            piece = y[r : r + 8, :]
            for j in range(t + 1):
                accs[j] = accs[j] + narrow(basis[j, r : r + 8, :] * piece)
        heights = [total(acc) for acc in accs]
        row = row_ref[...]
        for j in range(t + 1):
            row = jnp.where(lane == t * KRYLOV + j, heights[j], row)
        if t + 1 < KRYLOV:
            acc = jnp.zeros((8, 128), F32)
            for r in range(0, block, 8):
                rest = y[r : r + 8, :]
                for j in range(t + 1):
                    rest = rest - heights[j] * basis[j, r : r + 8, :]
                y[r : r + 8, :] = rest
                acc = acc + narrow(rest * rest)
            square = total(acc)
            scale = jnp.where(square > 0.0, lax.rsqrt(square), 0.0)
            for r in range(0, block, 16):
                new = y[r : r + 16, :] * scale
                basis[t + 1, r : r + 16, :] = new
                x[r : r + 16, :] = new.astype(BF16)
            row = jnp.where(lane == t * KRYLOV + t + 1, square * scale, row)
        row_ref[...] = row

    def krylov_step(t, _):
        apply()
        for i in range(KRYLOV):
            pl.when(t == i)(functools.partial(orthogonalize, i))
        return 0

    lax.fori_loop(0, KRYLOV, krylov_step, 0)

    home = group * SIDE + line
    table[home, pl.ds(place, 1), :] = row_ref[...]

    def copy_a(k, slot):
        piece = table.at[home, pl.ds(slot, 1), :]
        other = line * near + lax.rem(place + k, near)
        return remote(piece, piece, send_a.at[k], recv_a.at[slot], (group, other))

    def copy_b(k, slot):
        piece = table.at[group * SIDE + slot]
        other = lax.rem(line + k, SIDE) * near + place
        return remote(piece, piece, send_b.at[k], recv_b.at[slot], (group, other))

    def copy_c(k, slot):
        piece = table.at[pl.ds(slot * SIDE, SIDE)]
        return remote(piece, piece, send_c.at[k], recv_c.at[slot], (lax.rem(group + k, groups), me))

    for k in range(1, near):
        copy_a(k, place).start()
    for k in range(1, near):
        copy_a(k, lax.rem(place + k, near)).wait_recv()
    for k in range(1, SIDE):
        copy_b(k, line).start()
    for k in range(1, SIDE):
        copy_b(k, lax.rem(line + k, SIDE)).wait_recv()
    for k in range(1, groups):
        copy_c(k, group).start()
    for k in range(1, groups):
        copy_c(k, lax.rem(group + k, groups)).wait_recv()

    entries = table[...].reshape(groups * n, 128).T
    columns = [entries[t * KRYLOV : (t + 1) * KRYLOV, :] for t in range(KRYLOV)]
    norms = entries[64:65, :]
    sub = lax.broadcasted_iota(jnp.int32, (KRYLOV, 128), 0)
    lanes = lax.broadcasted_iota(jnp.int32, (KRYLOV, 128), 1)
    vectors = [jnp.where(sub == 0, norms / jnp.sqrt(total(norms * norms) + EPS), 0.0)]
    hess = jnp.zeros((KRYLOV, 128), F32)
    for t in range(KRYLOV):
        now = vectors[t]
        applied = columns[0] * now[0:1, :]
        for i in range(1, t + 1):
            applied = applied + columns[i] * now[i : i + 1, :]
        heights = [total(vectors[j] * applied) for j in range(t + 1)]
        for j in range(t + 1):
            hess = jnp.where((sub == j) & (lanes == t), heights[j], hess)
        if t + 1 < KRYLOV:
            rest = applied
            for j in range(t + 1):
                rest = rest - heights[j] * vectors[j]
            beta = jnp.sqrt(total(rest * rest) + EPS)
            hess = jnp.where((sub == t + 1) & (lanes == t), beta, hess)
            vectors.append(rest / beta)
    hess_ref[...] = hess[:, :KRYLOV]

    scaled = (-TAU / 16.0) * hess
    power = jnp.where(sub == lanes, 1.0, 0.0).astype(F32)
    series = power
    for order in range(1, 11):
        power = multiply(power, scaled) / float(order)
        series = series + power
    for _ in range(4):
        series = multiply(series, series)
    coefficients = series[:, 0:1]
    length = float(groups * n * block * wide)
    rescale = jnp.sqrt(jnp.full((1, 1), length, F32)) / jnp.sqrt(
        jnp.sum(coefficients * coefficients, axis=0, keepdims=True)
    )
    mixed = coefficients[0:1, :] * vectors[0]
    for t in range(1, KRYLOV):
        mixed = mixed + coefficients[t : t + 1, :] * vectors[t]
    weight = jnp.sum(jnp.where(lanes == group * n + me, mixed, 0.0), axis=1, keepdims=True) * rescale
    for p in range(phys):
        columns_p = slice(p * block, (p + 1) * block)
        acc = weight[0:1, :] * basis[0, :, columns_p]
        for j in range(1, KRYLOV):
            acc = acc + weight[j : j + 1, :] * basis[j, :, columns_p]
        out_ref[pl.ds(p, block, stride=phys), :] = acc

    def finish(peer):
        tell(peer, me).wait_send()
        spread_left(peer, me).wait_send()
        spread_right(peer, me).wait_send()
        route_left(peer, me).wait_send()
        for h in range(HALVES):
            route_right(h, peer, me).wait_send()

    each_peer(finish)
    for k in range(1, groups):
        panel_copy(k, group).wait_send()
        copy_c(k, group).wait_send()
    for k in range(1, SIDE):
        copy_b(k, line).wait_send()
    for k in range(1, near):
        copy_a(k, place).wait_send()


def local(state, panel, left_env, right_env, left_match, right_match, phys_states):
    n, groups = lax.axis_size("sector"), lax.axis_size("group")
    channels, block = left_env.shape[1], left_env.shape[2]
    phys = phys_states.shape[1]
    wide = phys * block
    rows = state.reshape(-1, state.shape[-1])
    vmem = pl.BlockSpec(memory_space=pltpu.VMEM)
    smem = pl.BlockSpec(memory_space=pltpu.SMEM)
    whole = pl.BlockSpec(memory_space=pl.ANY)
    piece = (n, block, block)
    dma = pltpu.SemaphoreType.DMA
    new_state, hessenberg = pl.pallas_call(
        kernel,
        out_shape=(
            jax.ShapeDtypeStruct(rows.shape, F32),
            jax.ShapeDtypeStruct((KRYLOV, KRYLOV), F32),
        ),
        in_specs=[smem, smem, smem, vmem, vmem, whole, whole],
        out_specs=(vmem, vmem),
        scratch_shapes=[
            pltpu.VMEM(piece, BF16),
            pltpu.VMEM(piece, BF16),
            pltpu.VMEM(piece, BF16),
            pltpu.VMEM(piece, BF16),
            pltpu.VMEM(piece, BF16),
            pltpu.VMEM(piece, BF16),
            pltpu.VMEM(piece, BF16),
            pltpu.VMEM(piece, BF16),
            pltpu.VMEM((n, 1, 128), jnp.int32),
            pltpu.SMEM((n, 1, 128), jnp.int32),
            pltpu.VMEM((groups,) + panel.shape, BF16),
            pltpu.VMEM((phys * phys, channels * channels), F32),
            pltpu.VMEM((phys, channels * phys * 8, channels * 8), BF16),
            pltpu.VMEM((channels * phys, block, wide), BF16),
            pltpu.VMEM((block, channels * block), BF16),
            pltpu.VMEM((channels, block, wide), BF16),
            pltpu.VMEM((block, wide), BF16),
            pltpu.VMEM((block, wide), F32),
            pltpu.VMEM((KRYLOV, block, wide), F32),
            pltpu.VMEM((1, 128), F32),
            pltpu.VMEM((groups * SIDE, 2 * SIDE, 128), F32),
            dma((3,)),
        ]
        + [dma((n,))] * 8
        + [dma((HALVES, n))] * 2
        + [dma((groups,))] * 2
        + [dma((2 * SIDE,))] * 2
        + [dma((SIDE,))] * 2
        + [dma((groups,))] * 2,
        compiler_params=pltpu.CompilerParams(collective_id=0, has_side_effects=True, vmem_limit_bytes=VMEM_LIMIT),
        name="step",
    )(left_match, right_match, phys_states, rows, panel, left_env[0], right_env[0])
    return new_state.reshape(state.shape), hessenberg


def solution(mesh):
    return jax.shard_map(
        local,
        mesh=mesh,
        in_specs=(
            P(("group", "sector"), None, None, None),
            P("group", None, None),
            P(("group", "sector"), None, None, None),
            P(("group", "sector"), None, None, None),
            P(("group", "sector")),
            P(("group", "sector")),
            P(("group", "sector"), None),
        ),
        out_specs=(P(("group", "sector"), None, None, None), P()),
        check_vma=False,
    )
```

time: 1440 us -> 110 us (0.08)
  blocking collectives: 1040 us -> 0 us
  matrix products: 142 us -> 0 us
  local copies, waits for them, and re-layouts: 110 us -> 2.27 us
  Pallas kernels: 0 us -> 104 us
  other arithmetic: 81.1 us -> 0 us
  starting transfers between devices: 27.1 us -> 0 us
    psum x16 -> x0, blocking collectives: 1020 us -> none  [the longest x8 504 us: local(): projection = lax.psum(local_projection, ('group', 'sector'))]
    dot_general x55 -> x0, matrix products: 142 us -> none  [the longest x8 47.6 us: apply_sector(): jnp.einsum('aiqj,aqcp->cipj', inner, mixing, preferred_element_type=jnp.f...]
    pallas_call x0 -> x1, Pallas kernels: none -> 104 us  [local(): pl.pallas_call(kernel, out_shape=(jax.ShapeDtypeStruct(rows.shape, F32),...]
    another operation x9 -> x0, local copies, waits for them, and re-layouts: 55.6 us -> none
    unnamed x2 -> x0, other arithmetic: 45.8 us -> none
    scatter x23 -> x0, local copies, waits for them, and re-layouts: 28.4 us -> none  [the longest x7 26.8 us: local(): krylov_basis = krylov_basis.at[column + 1].set(remainder / subdiag)]
    all_to_all x4 -> x0, starting transfers between devices: 27.1 us -> none  [the longest x1 9.6 us: local(): lax.all_to_all(left_rows, 'sector', split_axis=1, concat_axis=0, tiled=True)]
  transfers between devices with their start and end apart: 4 -> 0, of which waited for: 1 -> 0; matrix products, arithmetic and copies ran while one was open for 5% -> 0% of each run, Pallas kernels for 0% -> 0%
where the time goes in v2:
time: 110 us; the launch traced here: 109 us
  Pallas kernels  104 us (95%)
  local copies, waits for them, and re-layouts  2.27 us (2%)
  between operations  1.94 us (2%)
    pallas_call x1, Pallas kernels, local(): pl.pallas_call(kernel, out_shape=(jax.ShapeDtypeStruct(rows.shape, F32),...  104 us
    unnamed x4, local copies, waits for them, and re-layouts  2.27 us

profile of v2, /device:TPU:1, one launch (start us, length us, event | category | flops | bytes accessed | tf_op | source)
XLA Modules:
  0.0 108.6 jit_solution(6492790219318302233)
XLA Ops:
  1.9 104.4 %step.1 = (f32[512,128]{1,0:T(8,128)}, f32[8,8]{1,0:T(8,128)}) custom-call(s32[1]{0:T(128)S(6)} %copy.11.lm_ref, s32[1]{0:T(128)S(6)} %copy.12.rm_ref, s32[1,4]{1,0:T(1,128)} %states_ref.1, f32[512,128]{1,0:T(8,128)} %bitcast.6, bf16[8,32,256]{2,1,0:T(8,128)(2,1)} %panel_ref.1, bf16[32,128,128]{2,1,0:T(8,128)(2,1)} %bitcast.4, bf16[32,128,128]{2,1,0:T(8,128)(2,1)} %bitcast.5), custom_call_target="tpu_custom_call" | custom-call | tf_op jit(solution)/shard_map/step/pallas_call | solution.py:379
  106.4 0.0 copy-start
  106.4 1.7 %copy.13 = f32[1,128,4,128]{3,2,1,0:T(4,128)} copy(f32[1,128,4,128]{3,2,1,0:T(4,128)} %bitcast.7) | data formatting | bytes 524288
  108.0 0.0 copy-done
  108.0 0.6 copy.14
Async XLA Ops:
  106.4 1.7 %copy-start = (f32[8,8]{1,0:T(8,128)S(1)}, f32[8,8]{1,0:T(8,128)}, u32[]{:S(2)}) copy-start(f32[8,8]{1,0:T(8,128)} %get-tuple-element.9) | copy-start | bytes 772

commit v3 on v2

--- a/solution.py
+++ b/solution.py
@@ -1,4 +1,5 @@
 import functools
+import math
 
 import jax
 import jax.numpy as jnp
@@ -16,7 +17,6 @@
 EPS = 1e-06
 VMEM_LIMIT = 56 * 1024 * 1024
 SIDE = 4
-HALVES = 2
 
 
 def far_first():
@@ -52,12 +52,12 @@
 
 
 def kernel(
-    lm_ref, rm_ref, states_ref, state_ref, panel_ref, left_ref, right_ref,
+    lm_any, rm_any, states_any, state_any, panel_any, left_ref, right_ref,
     out_ref, hess_ref,
-    right_v, turned, spread_l, spread_r, stage_l, stage_r, left_in, right_in, match_v, match_s, panels,
-    chosen, grown, joint, left_w, z, x, y, basis, row_ref, table,
+    lm_ref, rm_ref, states_ref, state_ref, right_v, turned, spread_l, spread_r, stage_l, stage_r, left_in, right_in, match_v, match_s, panels,
+    chosen, grown, joint, left_w, z, x, y, basis, squares, row_ref, last_ref, table, last_table,
     own_sem, send_m, recv_m, send_l, recv_l, send_r, recv_r, send_l2, recv_l2, send_r2, recv_r2,
-    send_p, recv_p, send_a, recv_a, send_b, recv_b, send_c, recv_c,
+    send_p, recv_p, send_a, recv_a, send_b, recv_b, send_c, recv_c, send_d, recv_d,
 ):
     group = lax.axis_index("group")
     me = lax.axis_index("sector")
@@ -74,6 +74,9 @@
         dy, dz, dc = offset
         return lax.rem(line + dy, SIDE) * near + lax.rem(chip + dz, SIDE) * 2 + lax.rem(core + dc, 2)
 
+    def back(offset):
+        return at((-offset[0] % SIDE, -offset[1] % SIDE, offset[2]))
+
     def each_peer(body):
         def step(k, _):
             body(lax.rem(me + k, n))
@@ -84,16 +87,31 @@
     barrier = pltpu.get_barrier_semaphore()
     each_peer(lambda peer: pl.semaphore_signal(barrier, inc=1, device_id=(group, peer), device_id_type=MESH))
     for k in range(1, groups):
-        pl.semaphore_signal(barrier, inc=1, device_id=(lax.rem(group + k, groups), me), device_id_type=MESH)
-
-    load_r = pltpu.make_async_copy(right_ref, right_v, own_sem.at[0])
-    keep_l = pltpu.make_async_copy(left_ref.at[me], spread_l.at[me], own_sem.at[1])
-    load_r.start()
-    keep_l.start()
-    panels[group] = panel_ref[...]
+        for step in range(SIDE):
+            other = lax.rem(line + step, SIDE) * near + place
+            pl.semaphore_signal(barrier, inc=1, device_id=(lax.rem(group + k, groups), other), device_id_type=MESH)
+
+    loads = [
+        pltpu.make_async_copy(src, dst, own_sem.at[i])
+        for i, (src, dst) in enumerate(
+            (
+                (right_ref, right_v),
+                (left_ref.at[me], spread_l.at[me]),
+                (panel_any, panels.at[group]),
+                (lm_any, lm_ref),
+                (rm_any, rm_ref),
+                (states_any, states_ref),
+                (state_any, state_ref),
+            )
+        )
+    ]
+    for load in loads:
+        load.start()
+    for load in loads[:5]:
+        load.wait()
     lane = lax.broadcasted_iota(jnp.int32, (1, 128), 1)
     match_v[me] = jnp.where(lane == 0, lm_ref[0], rm_ref[0])
-    pl.semaphore_wait(barrier, n - 1 + groups - 1)
+    pl.semaphore_wait(barrier, n - 1 + (groups - 1) * SIDE)
 
     def remote(src, dst, send, recv, device):
         return pltpu.make_async_remote_copy(
@@ -112,13 +130,8 @@
     def route_left(peer, slot):
         return remote(stage_l.at[peer], left_in.at[slot], send_l2.at[peer], recv_l2.at[slot], (group, peer))
 
-    part = block // HALVES
-
-    def route_right(h, peer, slot):
-        rows = pl.ds(h * part, part)
-        return remote(
-            stage_r.at[peer, rows], right_in.at[slot, rows], send_r2.at[h, peer], recv_r2.at[h, slot], (group, peer)
-        )
+    def route_right(peer, slot):
+        return remote(stage_r.at[peer], right_in.at[slot], send_r2.at[peer], recv_r2.at[slot], (group, peer))
 
     def panel_copy(k, slot):
         other = lax.rem(group + k, groups)
@@ -126,11 +139,6 @@
 
     for offset in ORDER:
         tell(at(offset), me).start()
-    for offset in ORDER:
-        spread_left(at(offset), me).start()
-    for k in range(1, groups):
-        panel_copy(k, group).start()
-    load_r.wait()
 
     def turn(peer):
         turned[peer] = right_v[peer].astype(F32).T.astype(BF16)
@@ -139,8 +147,15 @@
         peer = at(offset)
         turn(peer)
         spread_right(peer, me).start()
-    spread_r[me] = right_v[me].astype(F32).T.astype(BF16)
-
+    for k in range(1, groups):
+        panel_copy(k, group).start()
+    for offset in ORDER:
+        spread_left(at(offset), me).start()
+    turn(me)
+    spread_r[me] = turned[me]
+
+    loads[5].wait()
+    loads[6].wait()
     big = jnp.max(jnp.max(jnp.abs(state_ref[...]), axis=0, keepdims=True), axis=1, keepdims=True)
     shrink = jnp.where(big > 0.0, 1.0 / big, 0.0)
     for q in range(phys):
@@ -151,11 +166,16 @@
         acc = acc + narrow(piece * piece)
     size = jnp.sqrt(total(acc))
     scale = jnp.where(size > 0.0, 1.0 / size, 0.0)
+    acc_first = jnp.zeros((8, 128), F32)
     for r in range(0, block, 16):
         first = y[r : r + 16, :] * scale
         basis[0, r : r + 16, :] = first
         x[r : r + 16, :] = first.astype(BF16)
+        acc_first = acc_first + narrow(first[:8] * first[:8]) + narrow(first[8:] * first[8:])
+    own_square = total(acc_first)
+    squares[0:1, :] = jnp.broadcast_to(own_square, (1, 128))
     row_ref[...] = jnp.where(lane == 64, big * size, 0.0)
+    last_ref[...] = jnp.zeros((1, 128), F32)
 
     for k in range(1, groups):
         panel_copy(k, lax.rem(group + k, groups)).wait_recv()
@@ -186,29 +206,24 @@
         grown[p] = jnp.where(same, wider[:, None, :], 0.0).reshape(channels * phys * 8, 8 * channels).astype(BF16)
 
     each_peer(lambda peer: tell(peer, peer).wait_recv())
-    to_scalar = pltpu.make_async_copy(match_v, match_s, own_sem.at[2])
+    to_scalar = pltpu.make_async_copy(match_v, match_s, own_sem.at[7])
     to_scalar.start()
-    keep_l.wait()
     to_scalar.wait()
+    each_peer(lambda peer: spread_right(peer, peer).wait_recv())
+    for offset in ORDER:
+        peer = at(offset)
+        stage_r[peer] = spread_r[match_s[peer, 0, 1]]
+        route_right(peer, me).start()
+    right_in[me] = spread_r[match_s[me, 0, 1]]
+
     each_peer(lambda peer: spread_left(peer, peer).wait_recv())
     for offset in ORDER:
         peer = at(offset)
+        source = back(offset)
+        route_right(source, source).wait_recv()
         stage_l[peer] = spread_l[match_s[peer, 0, 0]]
         route_left(peer, me).start()
     left_in[me] = spread_l[match_s[me, 0, 0]]
-
-    each_peer(lambda peer: spread_right(peer, peer).wait_recv())
-    for h in range(HALVES):
-        for offset in ORDER:
-            peer = at(offset)
-            if h == 0:
-                stage_r[peer] = spread_r[match_s[peer, 0, 1]]
-            route_right(h, peer, me).start()
-    right_in[me] = spread_r[match_s[me, 0, 1]]
-
-    each_peer(lambda peer: route_left(peer, peer).wait_recv())
-    for a in range(channels):
-        left_w[:, a * block : (a + 1) * block] = left_in[a]
 
     def join(m, _):
         start = pl.multiple_of(m * 16, 16)
@@ -224,111 +239,149 @@
             ).astype(BF16)
         return 0
 
-    for h in range(HALVES):
-        each_peer(lambda peer: route_right(h, peer, peer).wait_recv())
-        lax.fori_loop(h * part // 16, (h + 1) * part // 16, join, 0)
-
-    def apply():
+    lax.fori_loop(0, block // 16, join, 0)
+
+    def right_product():
         for a in range(channels):
             weights = joint[a * phys : (a + 1) * phys].reshape(wide, wide)
             z[a] = jnp.dot(x[...], weights, preferred_element_type=F32).astype(BF16)
+
+    def left_product():
         y[...] = jnp.dot(left_w[...], z[...].reshape(channels * block, wide), preferred_element_type=F32)
+
+    right_product()
+    each_peer(lambda peer: route_left(peer, peer).wait_recv())
+    for a in range(channels):
+        left_w[:, a * block : (a + 1) * block] = left_in[a]
 
     def orthogonalize(t):
         accs = [jnp.zeros((8, 128), F32)] * (t + 1)
+        whole = jnp.zeros((8, 128), F32)
         for r in range(0, block, 8):
             piece = y[r : r + 8, :]
             for j in range(t + 1):
                 accs[j] = accs[j] + narrow(basis[j, r : r + 8, :] * piece)
-        heights = [total(acc) for acc in accs]
-        row = row_ref[...]
+            whole = whole + narrow(piece * piece)
+        heights = []
+        for j in range(t + 1):
+            square = squares[j : j + 1, 0:1]
+            heights.append(total(accs[j]) * jnp.where(square > 0.0, 1.0 / square, 0.0))
+        target = last_ref if t + 1 == KRYLOV else row_ref
+        row = target[...]
         for j in range(t + 1):
             row = jnp.where(lane == t * KRYLOV + j, heights[j], row)
         if t + 1 < KRYLOV:
+            size = total(whole)
+            scale = jnp.where(size > 0.0, lax.rsqrt(size), 0.0)
             acc = jnp.zeros((8, 128), F32)
-            for r in range(0, block, 8):
-                rest = y[r : r + 8, :]
+            for r in range(0, block, 16):
+                rest = y[r : r + 16, :]
                 for j in range(t + 1):
-                    rest = rest - heights[j] * basis[j, r : r + 8, :]
-                y[r : r + 8, :] = rest
-                acc = acc + narrow(rest * rest)
-            square = total(acc)
-            scale = jnp.where(square > 0.0, lax.rsqrt(square), 0.0)
-            for r in range(0, block, 16):
-                new = y[r : r + 16, :] * scale
-                basis[t + 1, r : r + 16, :] = new
-                x[r : r + 16, :] = new.astype(BF16)
-            row = jnp.where(lane == t * KRYLOV + t + 1, square * scale, row)
-        row_ref[...] = row
+                    rest = rest - heights[j] * basis[j, r : r + 16, :]
+                rest = rest * scale
+                basis[t + 1, r : r + 16, :] = rest
+                x[r : r + 16, :] = rest.astype(BF16)
+                rest = rest * rest
+                acc = acc + (narrow(rest[:8]) + narrow(rest[8:]))
+            squares[t + 1 : t + 2, :] = jnp.broadcast_to(total(acc), (1, 128))
+            row = jnp.where(lane == t * KRYLOV + t + 1, size * scale, row)
+        target[...] = row
 
     def krylov_step(t, _):
-        apply()
-        for i in range(KRYLOV):
+        left_product()
+        for i in range(KRYLOV - 1):
             pl.when(t == i)(functools.partial(orthogonalize, i))
+        pl.when(t + 2 < KRYLOV)(right_product)
         return 0
 
-    lax.fori_loop(0, KRYLOV, krylov_step, 0)
+    lax.fori_loop(0, KRYLOV - 1, krylov_step, 0)
 
     home = group * SIDE + line
-    table[home, pl.ds(place, 1), :] = row_ref[...]
-
-    def copy_a(k, slot):
-        piece = table.at[home, pl.ds(slot, 1), :]
+    lines = groups * SIDE
+
+    def near_copy(rows, send, recv, k, slot):
+        piece = rows.at[home, pl.ds(slot, 1), :]
         other = line * near + lax.rem(place + k, near)
-        return remote(piece, piece, send_a.at[k], recv_a.at[slot], (group, other))
-
-    def copy_b(k, slot):
-        piece = table.at[group * SIDE + slot]
-        other = lax.rem(line + k, SIDE) * near + place
-        return remote(piece, piece, send_b.at[k], recv_b.at[slot], (group, other))
-
-    def copy_c(k, slot):
-        piece = table.at[pl.ds(slot * SIDE, SIDE)]
-        return remote(piece, piece, send_c.at[k], recv_c.at[slot], (lax.rem(group + k, groups), me))
-
+        return remote(piece, piece, send.at[k], recv.at[slot], (group, other))
+
+    def far_copy(rows, send, recv, k, slot):
+        piece = rows.at[slot]
+        other = lax.rem(home + k, lines)
+        return remote(piece, piece, send.at[k], recv.at[slot], (other // SIDE, lax.rem(other, SIDE) * near + place))
+
+    first_near = functools.partial(near_copy, table, send_a, recv_a)
+    first_far = functools.partial(far_copy, table, send_b, recv_b)
+    last_near = functools.partial(near_copy, last_table, send_c, recv_c)
+    last_far = functools.partial(far_copy, last_table, send_d, recv_d)
+
+    row = row_ref[...]
+    for j in range(KRYLOV):
+        row = jnp.where(lane == 72 + j, squares[j : j + 1, :], row)
+    table[home, pl.ds(place, 1), :] = row
     for k in range(1, near):
-        copy_a(k, place).start()
+        first_near(k, place).start()
+    right_product()
+    left_product()
+    orthogonalize(KRYLOV - 1)
+    last_table[home, pl.ds(place, 1), :] = last_ref[...]
     for k in range(1, near):
-        copy_a(k, lax.rem(place + k, near)).wait_recv()
-    for k in range(1, SIDE):
-        copy_b(k, line).start()
-    for k in range(1, SIDE):
-        copy_b(k, lax.rem(line + k, SIDE)).wait_recv()
-    for k in range(1, groups):
-        copy_c(k, group).start()
-    for k in range(1, groups):
-        copy_c(k, lax.rem(group + k, groups)).wait_recv()
+        last_near(k, place).start()
+    for k in range(1, near):
+        first_near(k, lax.rem(place + k, near)).wait_recv()
+    for k in range(1, lines):
+        first_far(k, home).start()
+    for k in range(1, near):
+        last_near(k, lax.rem(place + k, near)).wait_recv()
+    for k in range(1, lines):
+        last_far(k, home).start()
+    for k in range(1, lines):
+        first_far(k, lax.rem(home + k, lines)).wait_recv()
 
     entries = table[...].reshape(groups * n, 128).T
-    columns = [entries[t * KRYLOV : (t + 1) * KRYLOV, :] for t in range(KRYLOV)]
+    columns = [entries[t * KRYLOV : (t + 1) * KRYLOV, :] for t in range(KRYLOV - 1)]
     norms = entries[64:65, :]
+    metric = entries[72:80, :]
     sub = lax.broadcasted_iota(jnp.int32, (KRYLOV, 128), 0)
     lanes = lax.broadcasted_iota(jnp.int32, (KRYLOV, 128), 1)
     vectors = [jnp.where(sub == 0, norms / jnp.sqrt(total(norms * norms) + EPS), 0.0)]
+    duals = [vectors[0] * metric]
     hess = jnp.zeros((KRYLOV, 128), F32)
-    for t in range(KRYLOV):
+
+    def advance(t, hess):
         now = vectors[t]
         applied = columns[0] * now[0:1, :]
         for i in range(1, t + 1):
             applied = applied + columns[i] * now[i : i + 1, :]
-        heights = [total(vectors[j] * applied) for j in range(t + 1)]
+        heights = [total(duals[j] * applied) for j in range(t + 1)]
         for j in range(t + 1):
             hess = jnp.where((sub == j) & (lanes == t), heights[j], hess)
         if t + 1 < KRYLOV:
             rest = applied
             for j in range(t + 1):
                 rest = rest - heights[j] * vectors[j]
-            beta = jnp.sqrt(total(rest * rest) + EPS)
+            beta = jnp.sqrt(total(rest * rest * metric) + EPS)
             hess = jnp.where((sub == t + 1) & (lanes == t), beta, hess)
             vectors.append(rest / beta)
+            duals.append(vectors[t + 1] * metric)
+        return hess
+
+    for t in range(KRYLOV - 1):
+        hess = advance(t, hess)
+    for k in range(1, lines):
+        last_far(k, lax.rem(home + k, lines)).wait_recv()
+    columns.append(last_table[...].reshape(groups * n, 128).T[56:64, :])
+    hess = advance(KRYLOV - 1, hess)
     hess_ref[...] = hess[:, :KRYLOV]
 
     scaled = (-TAU / 16.0) * hess
-    power = jnp.where(sub == lanes, 1.0, 0.0).astype(F32)
-    series = power
-    for order in range(1, 11):
-        power = multiply(power, scaled) / float(order)
-        series = series + power
+    unit = jnp.where(sub == lanes, 1.0, 0.0).astype(F32)
+    second = multiply(scaled, scaled)
+    third = multiply(second, scaled)
+    inverse = [1.0 / math.factorial(order) for order in range(11)]
+    series = inverse[9] * unit + inverse[10] * scaled
+    for order in (6, 3, 0):
+        lower = inverse[order] * unit + inverse[order + 1] * scaled + inverse[order + 2] * second
+        series = lower + multiply(third, series)
     for _ in range(4):
         series = multiply(series, series)
     coefficients = series[:, 0:1]
@@ -345,24 +398,30 @@
         acc = weight[0:1, :] * basis[0, :, columns_p]
         for j in range(1, KRYLOV):
             acc = acc + weight[j : j + 1, :] * basis[j, :, columns_p]
-        out_ref[pl.ds(p, block, stride=phys), :] = acc
+        out_ref[p] = acc
 
     def finish(peer):
         tell(peer, me).wait_send()
         spread_left(peer, me).wait_send()
         spread_right(peer, me).wait_send()
         route_left(peer, me).wait_send()
-        for h in range(HALVES):
-            route_right(h, peer, me).wait_send()
+        route_right(peer, me).wait_send()
 
     each_peer(finish)
     for k in range(1, groups):
         panel_copy(k, group).wait_send()
-        copy_c(k, group).wait_send()
-    for k in range(1, SIDE):
-        copy_b(k, line).wait_send()
     for k in range(1, near):
-        copy_a(k, place).wait_send()
+        first_near(k, place).wait_send()
+        last_near(k, place).wait_send()
+    for k in range(1, lines):
+        first_far(k, home).wait_send()
+        last_far(k, home).wait_send()
+
+
+def finish_kernel(parts_ref, matrix_ref, state_out, hess_out):
+    for p in range(parts_ref.shape[0]):
+        state_out[:, p, :] = parts_ref[p]
+    hess_out[...] = matrix_ref[...]
 
 
 def local(state, panel, left_env, right_env, left_match, right_match, phys_states):
@@ -372,19 +431,22 @@
     wide = phys * block
     rows = state.reshape(-1, state.shape[-1])
     vmem = pl.BlockSpec(memory_space=pltpu.VMEM)
-    smem = pl.BlockSpec(memory_space=pltpu.SMEM)
     whole = pl.BlockSpec(memory_space=pl.ANY)
     piece = (n, block, block)
     dma = pltpu.SemaphoreType.DMA
-    new_state, hessenberg = pl.pallas_call(
+    parts, matrix = pl.pallas_call(
         kernel,
         out_shape=(
-            jax.ShapeDtypeStruct(rows.shape, F32),
+            jax.ShapeDtypeStruct((phys, block, block), F32),
             jax.ShapeDtypeStruct((KRYLOV, KRYLOV), F32),
         ),
-        in_specs=[smem, smem, smem, vmem, vmem, whole, whole],
+        in_specs=[whole] * 7,
         out_specs=(vmem, vmem),
         scratch_shapes=[
+            pltpu.SMEM(left_match.shape, jnp.int32),
+            pltpu.SMEM(right_match.shape, jnp.int32),
+            pltpu.SMEM(phys_states.shape, jnp.int32),
+            pltpu.VMEM(rows.shape, F32),
             pltpu.VMEM(piece, BF16),
             pltpu.VMEM(piece, BF16),
             pltpu.VMEM(piece, BF16),
@@ -404,19 +466,32 @@
             pltpu.VMEM((block, wide), BF16),
             pltpu.VMEM((block, wide), F32),
             pltpu.VMEM((KRYLOV, block, wide), F32),
+            pltpu.VMEM((KRYLOV, 128), F32),
+            pltpu.VMEM((1, 128), F32),
             pltpu.VMEM((1, 128), F32),
             pltpu.VMEM((groups * SIDE, 2 * SIDE, 128), F32),
-            dma((3,)),
+            pltpu.VMEM((groups * SIDE, 2 * SIDE, 128), F32),
+            dma((8,)),
         ]
-        + [dma((n,))] * 8
-        + [dma((HALVES, n))] * 2
+        + [dma((n,))] * 10
         + [dma((groups,))] * 2
         + [dma((2 * SIDE,))] * 2
-        + [dma((SIDE,))] * 2
-        + [dma((groups,))] * 2,
+        + [dma((groups * SIDE,))] * 2
+        + [dma((2 * SIDE,))] * 2
+        + [dma((groups * SIDE,))] * 2,
         compiler_params=pltpu.CompilerParams(collective_id=0, has_side_effects=True, vmem_limit_bytes=VMEM_LIMIT),
         name="step",
     )(left_match, right_match, phys_states, rows, panel, left_env[0], right_env[0])
+    new_state, hessenberg = pl.pallas_call(
+        finish_kernel,
+        out_shape=(
+            jax.ShapeDtypeStruct(state.shape[1:], F32),
+            jax.ShapeDtypeStruct((KRYLOV, KRYLOV), F32),
+        ),
+        in_specs=[vmem, vmem],
+        out_specs=(vmem, vmem),
+        name="finish",
+    )(parts, matrix)
     return new_state.reshape(state.shape), hessenberg
 
 

time: 110 us -> 104 us (0.945); the launches traced: 109 us -> 104 us
  local copies, waits for them, and re-layouts: 2.27 us -> 0 us
  Pallas kernels: 104 us -> 102 us
    unnamed x4 -> x0, local copies, waits for them, and re-layouts: 2.27 us -> none
    pallas_call x1 -> x2, Pallas kernels: 104 us -> 102 us  [the longest x1 101 us: local(): pl.pallas_call(kernel, out_shape=(jax.ShapeDtypeStruct((phys, block, bloc...]
where the time goes in v3:
time: 104 us
  Pallas kernels  102 us (98%)
  between operations  1.93 us (2%)
    pallas_call x1, Pallas kernels, local(): pl.pallas_call(kernel, out_shape=(jax.ShapeDtypeStruct((phys, block, bloc...  101 us

profile of v3, /device:TPU:1, one launch (start us, length us, event | category | flops | bytes accessed | tf_op | source)
XLA Modules:
  0.0 104.3 jit_solution(16558978710162795065)
XLA Ops:
  1.9 100.6 %step.1 = (f32[4,128,128]{2,1,0:T(8,128)}, f32[8,8]{1,0:T(8,128)}) custom-call(s32[1]{0:T(128)S(6)} %copy.9.lm_any, s32[1]{0:T(128)S(6)} %copy.10.rm_any, s32[1,4]{1,0:T(1,128)} %states_any.1, f32[512,128]{1,0:T(8,128)} %bitcast.6, bf16[8,32,256]{2,1,0:T(8,128)(2,1)} %panel_any.1, bf16[32,128,128]{2,1,0:T(8,128)(2,1)} %bitcast.4, bf16[32,128,128]{2,1,0:T(8,128)(2,1)} %bitcast.5), custom_call_target="tpu_custom_call" | custom-call | tf_op jit(solution)/shard_map/step/pallas_call | solution.py:437
  102.5 1.8 %finish.1 = (f32[128,4,128]{2,1,0:T(4,128)}, f32[8,8]{1,0:T(8,128)}) custom-call(f32[4,128,128]{2,1,0:T(8,128)} %get-tuple-element.6.parts_ref, f32[8,8]{1,0:T(8,128)} %get-tuple-element.7.matrix_ref), custom_call_target="tpu_custom_call" | custom-call | tf_op jit(solution)/shard_map/finish/pallas_call | solution.py:485

commit v4 on v3

--- a/solution.py
+++ b/solution.py
@@ -15,6 +15,7 @@
 KRYLOV = 8
 TAU = 3.0
 EPS = 1e-06
+LEAD = 24
 VMEM_LIMIT = 56 * 1024 * 1024
 SIDE = 4
 
@@ -34,6 +35,8 @@
 
 
 ORDER = far_first()
+NEAR_STEPS = (4, 5, 3, 2, 6, 1, 7)
+FAR_STEPS = (10, 9, 11, 6, 14, 8, 2, 5, 7, 13, 15, 4, 12, 1, 3)
 
 
 def total(value):
@@ -52,9 +55,9 @@
 
 
 def kernel(
-    lm_any, rm_any, states_any, state_any, panel_any, left_ref, right_ref,
+    match_any, states_any, state_any, panel_any, left_ref, right_ref,
     out_ref, hess_ref,
-    lm_ref, rm_ref, states_ref, state_ref, right_v, turned, spread_l, spread_r, stage_l, stage_r, left_in, right_in, match_v, match_s, panels,
+    match_ref, states_ref, state_ref, right_v, turned, spread_l, spread_r, stage_l, stage_r, left_in, right_in, match_v, match_s, panels,
     chosen, grown, joint, left_w, z, x, y, basis, squares, row_ref, last_ref, table, last_table,
     own_sem, send_m, recv_m, send_l, recv_l, send_r, recv_r, send_l2, recv_l2, send_r2, recv_r2,
     send_p, recv_p, send_a, recv_a, send_b, recv_b, send_c, recv_c, send_d, recv_d,
@@ -98,8 +101,7 @@
                 (right_ref, right_v),
                 (left_ref.at[me], spread_l.at[me]),
                 (panel_any, panels.at[group]),
-                (lm_any, lm_ref),
-                (rm_any, rm_ref),
+                (match_any, match_ref),
                 (states_any, states_ref),
                 (state_any, state_ref),
             )
@@ -107,10 +109,10 @@
     ]
     for load in loads:
         load.start()
-    for load in loads[:5]:
+    for load in loads[:4]:
         load.wait()
     lane = lax.broadcasted_iota(jnp.int32, (1, 128), 1)
-    match_v[me] = jnp.where(lane == 0, lm_ref[0], rm_ref[0])
+    match_v[me] = jnp.where(lane == 0, match_ref[0, 0] // n, lax.rem(match_ref[0, 0], n))
     pl.semaphore_wait(barrier, n - 1 + (groups - 1) * SIDE)
 
     def remote(src, dst, send, recv, device):
@@ -149,13 +151,15 @@
         spread_right(peer, me).start()
     for k in range(1, groups):
         panel_copy(k, group).start()
-    for offset in ORDER:
+    for i, offset in enumerate(ORDER):
+        source = back(offset)
+        spread_right(source, source).wait_recv()
         spread_left(at(offset), me).start()
     turn(me)
     spread_r[me] = turned[me]
 
+    loads[4].wait()
     loads[5].wait()
-    loads[6].wait()
     big = jnp.max(jnp.max(jnp.abs(state_ref[...]), axis=0, keepdims=True), axis=1, keepdims=True)
     shrink = jnp.where(big > 0.0, 1.0 / big, 0.0)
     for q in range(phys):
@@ -209,7 +213,6 @@
     to_scalar = pltpu.make_async_copy(match_v, match_s, own_sem.at[7])
     to_scalar.start()
     to_scalar.wait()
-    each_peer(lambda peer: spread_right(peer, peer).wait_recv())
     for offset in ORDER:
         peer = at(offset)
         stage_r[peer] = spread_r[match_s[peer, 0, 1]]
@@ -217,10 +220,13 @@
     right_in[me] = spread_r[match_s[me, 0, 1]]
 
     each_peer(lambda peer: spread_left(peer, peer).wait_recv())
-    for offset in ORDER:
+    here = 0
+    for i, offset in enumerate(ORDER):
         peer = at(offset)
-        source = back(offset)
-        route_right(source, source).wait_recv()
+        while here < min(i + LEAD, len(ORDER)):
+            source = back(ORDER[here])
+            route_right(source, source).wait_recv()
+            here += 1
         stage_l[peer] = spread_l[match_s[peer, 0, 0]]
         route_left(peer, me).start()
     left_in[me] = spread_l[match_s[me, 0, 0]]
@@ -250,9 +256,20 @@
         y[...] = jnp.dot(left_w[...], z[...].reshape(channels * block, wide), preferred_element_type=F32)
 
     right_product()
-    each_peer(lambda peer: route_left(peer, peer).wait_recv())
-    for a in range(channels):
-        left_w[:, a * block : (a + 1) * block] = left_in[a]
+
+    sources = [me] + [back(offset) for offset in ORDER]
+    for start in range(0, n, 8):
+        batch = sources[start : start + 8]
+        for source in batch:
+            if source is not me:
+                route_left(source, source).wait_recv()
+            left_w[:, pl.ds(pl.multiple_of(source * block, block), block)] = left_in[source]
+        out = jnp.dot(
+            jnp.concatenate([left_in[source] for source in batch], axis=1),
+            jnp.concatenate([z[source] for source in batch], axis=0),
+            preferred_element_type=F32,
+        )
+        y[...] = out if start == 0 else y[...] + out
 
     def orthogonalize(t):
         accs = [jnp.zeros((8, 128), F32)] * (t + 1)
@@ -288,10 +305,14 @@
         target[...] = row
 
     def krylov_step(t, _):
-        left_product()
         for i in range(KRYLOV - 1):
             pl.when(t == i)(functools.partial(orthogonalize, i))
-        pl.when(t + 2 < KRYLOV)(right_product)
+
+        @pl.when(t + 2 < KRYLOV)
+        def _():
+            right_product()
+            left_product()
+
         return 0
 
     lax.fori_loop(0, KRYLOV - 1, krylov_step, 0)
@@ -318,21 +339,21 @@
     for j in range(KRYLOV):
         row = jnp.where(lane == 72 + j, squares[j : j + 1, :], row)
     table[home, pl.ds(place, 1), :] = row
-    for k in range(1, near):
+    for k in NEAR_STEPS:
         first_near(k, place).start()
     right_product()
     left_product()
     orthogonalize(KRYLOV - 1)
     last_table[home, pl.ds(place, 1), :] = last_ref[...]
-    for k in range(1, near):
+    for k in NEAR_STEPS:
         last_near(k, place).start()
     for k in range(1, near):
         first_near(k, lax.rem(place + k, near)).wait_recv()
-    for k in range(1, lines):
+    for k in FAR_STEPS:
         first_far(k, home).start()
     for k in range(1, near):
         last_near(k, lax.rem(place + k, near)).wait_recv()
-    for k in range(1, lines):
+    for k in FAR_STEPS:
         last_far(k, home).start()
     for k in range(1, lines):
         first_far(k, lax.rem(home + k, lines)).wait_recv()
@@ -398,7 +419,7 @@
         acc = weight[0:1, :] * basis[0, :, columns_p]
         for j in range(1, KRYLOV):
             acc = acc + weight[j : j + 1, :] * basis[j, :, columns_p]
-        out_ref[p] = acc
+        out_ref[:, p, :] = acc
 
     def finish(peer):
         tell(peer, me).wait_send()
@@ -418,10 +439,15 @@
         last_far(k, home).wait_send()
 
 
-def finish_kernel(parts_ref, matrix_ref, state_out, hess_out):
-    for p in range(parts_ref.shape[0]):
-        state_out[:, p, :] = parts_ref[p]
-    hess_out[...] = matrix_ref[...]
+def finish_kernel(state_in, matrix_in, state_out, matrix_out, sems):
+    copies = [
+        pltpu.make_async_copy(state_in, state_out, sems.at[0]),
+        pltpu.make_async_copy(matrix_in, matrix_out, sems.at[1]),
+    ]
+    for copy in copies:
+        copy.start()
+    for copy in copies:
+        copy.wait()
 
 
 def local(state, panel, left_env, right_env, left_match, right_match, phys_states):
@@ -433,18 +459,18 @@
     vmem = pl.BlockSpec(memory_space=pltpu.VMEM)
     whole = pl.BlockSpec(memory_space=pl.ANY)
     piece = (n, block, block)
+    matches = (left_match * n + right_match).reshape(1, 1)
     dma = pltpu.SemaphoreType.DMA
     parts, matrix = pl.pallas_call(
         kernel,
         out_shape=(
-            jax.ShapeDtypeStruct((phys, block, block), F32),
+            jax.ShapeDtypeStruct(state.shape[1:], F32),
             jax.ShapeDtypeStruct((KRYLOV, KRYLOV), F32),
         ),
-        in_specs=[whole] * 7,
+        in_specs=[whole] * 6,
         out_specs=(vmem, vmem),
         scratch_shapes=[
-            pltpu.SMEM(left_match.shape, jnp.int32),
-            pltpu.SMEM(right_match.shape, jnp.int32),
+            pltpu.SMEM((1, 1), jnp.int32),
             pltpu.SMEM(phys_states.shape, jnp.int32),
             pltpu.VMEM(rows.shape, F32),
             pltpu.VMEM(piece, BF16),
@@ -481,7 +507,7 @@
         + [dma((groups * SIDE,))] * 2,
         compiler_params=pltpu.CompilerParams(collective_id=0, has_side_effects=True, vmem_limit_bytes=VMEM_LIMIT),
         name="step",
-    )(left_match, right_match, phys_states, rows, panel, left_env[0], right_env[0])
+    )(matches, phys_states, rows, panel, left_env[0], right_env[0])
     new_state, hessenberg = pl.pallas_call(
         finish_kernel,
         out_shape=(
@@ -489,7 +515,8 @@
             jax.ShapeDtypeStruct((KRYLOV, KRYLOV), F32),
         ),
         in_specs=[vmem, vmem],
-        out_specs=(vmem, vmem),
+        out_specs=(whole, whole),
+        scratch_shapes=[dma((2,))],
         name="finish",
     )(parts, matrix)
     return new_state.reshape(state.shape), hessenberg

time: 104 us -> 101 us (0.971)
  Pallas kernels: 102 us -> 98.8 us
    pallas_call x1, Pallas kernels: 101 us -> 97.1 us  [local(): pl.pallas_call(kernel, out_shape=(jax.ShapeDtypeStruct(state.shape[1:], F...]
where the time goes in v4:
time: 101 us
  Pallas kernels  98.8 us (98%)
  between operations  2.09 us (2%)
    pallas_call x1, Pallas kernels, local(): pl.pallas_call(kernel, out_shape=(jax.ShapeDtypeStruct(state.shape[1:], F...  97.1 us

profile of v4, /device:TPU:1, one launch (start us, length us, event | category | flops | bytes accessed | tf_op | source)
XLA Modules:
  0.0 100.9 jit_solution(15350960280209856625)
XLA Ops:
  1.9 97.1 %step.1 = (f32[128,4,128]{2,1,0:T(4,128)}, f32[8,8]{1,0:T(8,128)}) custom-call(s32[1,1]{1,0:T(1,128)} %bitcast.match_any, s32[1,4]{1,0:T(1,128)} %states_any.1, f32[512,128]{1,0:T(8,128)} %bitcast.7, bf16[8,32,256]{2,1,0:T(8,128)(2,1)} %panel_any.1, bf16[32,128,128]{2,1,0:T(8,128)(2,1)} %bitcast.5, bf16[32,128,128]{2,1,0:T(8,128)(2,1)} %bitcast.6), custom_call_target="tpu_custom_call" | custom-call | tf_op jit(solution)/shard_map/step/pallas_call | solution.py:464
  99.1 1.7 %finish.1 = (f32[128,4,128]{2,1,0:T(4,128)}, f32[8,8]{1,0:T(8,128)}) custom-call(f32[128,4,128]{2,1,0:T(4,128)} %get-tuple-element.6.state_in, f32[8,8]{1,0:T(8,128)} %get-tuple-element.7.matrix_in), custom_call_target="tpu_custom_call" | custom-call | tf_op jit(solution)/shard_map/finish/pallas_call | solution.py:511

commit v5 on v4

--- a/solution.py
+++ b/solution.py
@@ -351,6 +351,17 @@
         first_near(k, lax.rem(place + k, near)).wait_recv()
     for k in FAR_STEPS:
         first_far(k, home).start()
+
+    def left_here(peer):
+        tell(peer, me).wait_send()
+        spread_left(peer, me).wait_send()
+        spread_right(peer, me).wait_send()
+        route_left(peer, me).wait_send()
+        route_right(peer, me).wait_send()
+
+    each_peer(left_here)
+    for k in range(1, groups):
+        panel_copy(k, group).wait_send()
     for k in range(1, near):
         last_near(k, lax.rem(place + k, near)).wait_recv()
     for k in FAR_STEPS:
@@ -388,6 +399,12 @@
 
     for t in range(KRYLOV - 1):
         hess = advance(t, hess)
+    for k in range(1, near):
+        first_near(k, place).wait_send()
+        last_near(k, place).wait_send()
+    for k in range(1, lines):
+        first_far(k, home).wait_send()
+        last_far(k, home).wait_send()
     for k in range(1, lines):
         last_far(k, lax.rem(home + k, lines)).wait_recv()
     columns.append(last_table[...].reshape(groups * n, 128).T[56:64, :])
@@ -420,23 +437,6 @@
         for j in range(1, KRYLOV):
             acc = acc + weight[j : j + 1, :] * basis[j, :, columns_p]
         out_ref[:, p, :] = acc
-
-    def finish(peer):
-        tell(peer, me).wait_send()
-        spread_left(peer, me).wait_send()
-        spread_right(peer, me).wait_send()
-        route_left(peer, me).wait_send()
-        route_right(peer, me).wait_send()
-
-    each_peer(finish)
-    for k in range(1, groups):
-        panel_copy(k, group).wait_send()
-    for k in range(1, near):
-        first_near(k, place).wait_send()
-        last_near(k, place).wait_send()
-    for k in range(1, lines):
-        first_far(k, home).wait_send()
-        last_far(k, home).wait_send()
 
 
 def finish_kernel(state_in, matrix_in, state_out, matrix_out, sems):

time: 101 us -> 101 us (level)
  no operation moved by 1% of the time
where the time goes in v5:
time: 101 us; the launch traced here: 100 us
  Pallas kernels  98.2 us (97%)
  between operations  2.09 us (2%)
    pallas_call x1, Pallas kernels, local(): pl.pallas_call(kernel, out_shape=(jax.ShapeDtypeStruct(state.shape[1:], F...  96.6 us

profile of v5, /device:TPU:1, one launch (start us, length us, event | category | flops | bytes accessed | tf_op | source)
XLA Modules:
  0.0 100.3 jit_solution(12376602010653268799)
XLA Ops:
  1.9 96.6 %step.1 = (f32[128,4,128]{2,1,0:T(4,128)}, f32[8,8]{1,0:T(8,128)}) custom-call(s32[1,1]{1,0:T(1,128)} %bitcast.match_any, s32[1,4]{1,0:T(1,128)} %states_any.1, f32[512,128]{1,0:T(8,128)} %bitcast.7, bf16[8,32,256]{2,1,0:T(8,128)(2,1)} %panel_any.1, bf16[32,128,128]{2,1,0:T(8,128)(2,1)} %bitcast.5, bf16[32,128,128]{2,1,0:T(8,128)(2,1)} %bitcast.6), custom_call_target="tpu_custom_call" | custom-call | tf_op jit(solution)/shard_map/step/pallas_call | solution.py:464
  98.5 1.7 %finish.1 = (f32[128,4,128]{2,1,0:T(4,128)}, f32[8,8]{1,0:T(8,128)}) custom-call(f32[128,4,128]{2,1,0:T(4,128)} %get-tuple-element.6.state_in, f32[8,8]{1,0:T(8,128)} %get-tuple-element.7.matrix_in), custom_call_target="tpu_custom_call" | custom-call | tf_op jit(solution)/shard_map/finish/pallas_call | solution.py:511
